TPU v7x, 32 devices: a whole 2x2x4 slice. The times are simulated.
32 devices in a mesh: rep: 2 (over y), dom: 4 (over z), slab: 2 (over x), half: 2 (over core).
Axes of the slice: x: 2, y: 2, z: 4, core: 2. Of those that a mesh axis runs over, the one named last changes fastest.
Arguments:
- leaf_multipoles: bfloat16 [81, 8192], P(None, ('rep', 'dom', 'slab', 'half')), parts along dimension 1, may hold values from -6 to 6
- translate: bfloat16 [316, 81, 81], replicated, may hold values from -0.0390625 to 0.0390625
- shift_up: bfloat16 [8, 81, 81], replicated, may hold values from -0.25 to 0.25
- shift_down: bfloat16 [8, 81, 81], replicated, may hold values from -0.625 to 0.625
- export_rows: int32 [32, 16, 32], P(('rep', 'dom', 'slab', 'half')), parts along dimension 0, may hold values from 0 to 255
- leaf_lists: int32 [316, 8192], P(None, ('rep', 'dom', 'slab', 'half')), parts along dimension 1, may hold values from 0 to 768, as said below
- coarse_lists: int32 [316, 1024], P(None, ('rep', 'dom', 'slab', 'half')), parts along dimension 1, may hold values from 0 to 512, as said below
- positions: float32 [3, 131072], P(None, ('rep', 'dom', 'slab', 'half')), parts along dimension 1, may hold values from 0 to 1
- charges: float32 [131072], P(('rep', 'dom', 'slab', 'half')), parts along dimension 0, may hold values from -0.3 to 0.3
- counts: int32 [8192], P(('rep', 'dom', 'slab', 'half')), parts along dimension 0, may hold values from 1 to 16
- near_lists: int32 [27, 8192], P(None, ('rep', 'dom', 'slab', 'half')), parts along dimension 1, may hold values from 0 to 288, as said below
Outputs:
- local_field: float32 [81, 8192], P(None, ('rep', 'dom', 'slab', 'half')), parts along dimension 1
- near_potential: float32 [131072], P(('rep', 'dom', 'slab', 'half')), parts along dimension 0
There are 2 independent parts, one for each index of `rep`. A program takes and returns all parts, laid end to end along the dimension named above; an argument that names none is the same for every part. Nothing has to cross between parts.
Inputs may be any that keep to these rules, and one draw needn't show every extreme that they name: `leaf_lists`: each device's entries are relative to that device; an imported entry of device r names a peer p with (p - r) mod 16 in 1 to 8 or in 8 to 15; 768 means no source. `coarse_lists`: 512 means no source. `near_lists`: each entry lies within 16 boxes of its target's local index shifted by 16, or is 288 for no tile.
All inputs are finite; a program needn't handle non-finite values.
Results may differ from a plain program's by a relative error of at most 0.0019.
Values may be sent and summed in bfloat16 or wider, within the bound.
A program may use at most 128 MiB of HBM per device.

v0:
```python
import jax
import jax.numpy as jnp
from jax import lax
from jax.sharding import PartitionSpec as P

HALO = 16


softening = 0.01
best = lax.Precision.HIGHEST


def padded(block, sides, width):
    for axis, dim in sides:
        count = lax.axis_size(axis)
        forward = [(i, i + 1) for i in range(count - 1)]
        backward = [(target, source) for source, target in forward]
        low = lax.ppermute(
            lax.slice_in_dim(block, block.shape[dim] - width, None, axis=dim), axis, forward
        )
        high = lax.ppermute(lax.slice_in_dim(block, 0, width, axis=dim), axis, backward)
        block = jnp.concatenate([low, block, high], axis=dim)
    return block


def near_sum(extended, targets, rows):

    def step(total, index):
        source = extended[:, index, :]
        dist = jnp.zeros(total.shape + (source.shape[2],), jnp.float32)
        for axis_id in range(3):
            diff = targets[axis_id][:, :, None] - source[axis_id][:, None, :]
            dist = dist + diff * diff
        return (total + jnp.sum(source[3][:, None, :] * lax.rsqrt(dist + softening), axis=2), None)

    start = jnp.zeros(targets.shape[1:], jnp.float32)
    return lax.scan(step, start, rows)[0]


def far_part(
    leaf_multipoles, translate, shift_up, shift_down, export_rows, leaf_lists, coarse_lists
):
    coeffs, boxes = leaf_multipoles.shape
    outgoing = leaf_multipoles[:, export_rows[0].reshape(-1)]
    arrived = lax.all_to_all(
        outgoing, ("dom", "slab", "half"), split_axis=1, concat_axis=1, tiled=True
    )
    sources = jnp.concatenate([leaf_multipoles, arrived, jnp.zeros((coeffs, 1), jnp.bfloat16)], 1)
    leaf_far = jnp.einsum(
        "okc,cob->kb", translate, sources[:, leaf_lists], preferred_element_type=jnp.float32
    )
    children = leaf_multipoles.reshape(coeffs, boxes // 8, 8)
    parents = jnp.einsum("ckm,mpc->kp", shift_up, children, preferred_element_type=jnp.float32)
    every_parent = lax.all_gather(parents, ("dom", "slab", "half"), axis=1, tiled=True)
    parent_ext = jnp.concatenate([every_parent, jnp.zeros((coeffs, 1), jnp.float32)], 1)
    coarse_local = jnp.einsum(
        "okc,cob->kb",
        translate.astype(jnp.float32),
        parent_ext[:, coarse_lists],
        precision=best,
        preferred_element_type=jnp.float32,
    )
    coarse_round = coarse_local.astype(jnp.bfloat16)
    down = jnp.einsum(
        "ckm,mp->kpc", shift_down, coarse_round, preferred_element_type=jnp.float32
    ).reshape(coeffs, boxes)
    return leaf_far + down


def near_part(positions, charges, counts, near_lists):
    boxes = counts.shape[0]
    slot_count = charges.shape[0] // boxes
    valid = (jnp.arange(slot_count, dtype=jnp.int32)[None, :] < counts[:, None]).astype(jnp.float32)
    q_eff = charges.reshape(boxes, slot_count) * valid
    packed = jnp.concatenate([positions, q_eff.reshape(1, boxes * slot_count)], 0)
    widened = padded(packed, ((("dom", "slab", "half"), 1),), HALO * slot_count)
    extended = jnp.concatenate(
        [
            widened.reshape(4, boxes + 2 * HALO, slot_count),
            jnp.zeros((4, 1, slot_count), jnp.float32),
        ],
        1,
    )
    targets = packed.reshape(4, boxes, slot_count)
    return (near_sum(extended, targets, near_lists) * valid).reshape(boxes * slot_count)


def body(
    leaf_multipoles,
    translate,
    shift_up,
    shift_down,
    export_rows,
    leaf_lists,
    coarse_lists,
    positions,
    charges,
    counts,
    near_lists,
):
    local_field = far_part(
        leaf_multipoles, translate, shift_up, shift_down, export_rows, leaf_lists, coarse_lists
    )
    near_potential = near_part(positions, charges, counts, near_lists)
    return (local_field, near_potential)


def solution(mesh):
    in_specs = (
        P(None, ("rep", "dom", "slab", "half")),
        P(),
        P(),
        P(),
        P(("rep", "dom", "slab", "half"), None, None),
        P(None, ("rep", "dom", "slab", "half")),
        P(None, ("rep", "dom", "slab", "half")),
        P(None, ("rep", "dom", "slab", "half")),
        P(("rep", "dom", "slab", "half")),
        P(("rep", "dom", "slab", "half")),
        P(None, ("rep", "dom", "slab", "half")),
    )
    out_specs = (P(None, ("rep", "dom", "slab", "half")), P(("rep", "dom", "slab", "half")))
    return jax.shard_map(body, mesh=mesh, in_specs=in_specs, out_specs=out_specs, check_vma=False)
```

profile of v0, /device:TPU:1, one launch (start us, length us, event | category | flops | bytes accessed | tf_op | source)
XLA Modules:
  0.0 469.7 jit_solution(10835987080693547992)
XLA Ops:
  0.6 0.9 copy.72
  1.6 0.8 reshape_squeeze.3
  2.4 1.9 gather_fusion.1
  4.3 7.3 %all-to-all-start = ((bf16[81,16,32]{0,2,1:T(8,128)(2,1)}), bf16[81,16,32]{0,2,1:T(8,128)(2,1)S(1)}, u32[]{:S(2)}, u32[]{:S(2)}) async-start(bf16[81,16,32]{0,2,1:T(8,128)(2,1)} %bitcast.2), calls=%async_computation | async-start | bytes 262144 | tf_op jit(solution)/shard_map/all_to_all | solution.py:45
  12.5 0.7 broadcast_select_fusion
  13.3 0.7 pad_maximum_fusion.3
  14.0 3.5 collective-permute-start
  17.5 1.9 collective-permute-start.1
  19.4 1.0 concatenate.25
  20.5 0.8 reshape.136
  21.3 1.0 compare_select_fusion.1
  22.4 1.1 convolution_bitcast_fusion.1
  23.5 22.5 %all_gather.3 = f32[81,512]{0,1:T(8,128)S(1)} all-gather(f32[81,32]{0,1:T(8,128)S(1)} %convolution_bitcast_fusion.1), channel_id=1, replica_groups=mesh['rep'=2,'dom'=4,'slab'=2,'half'=2] {'dom','slab','half'}, dimensions={1}, use_global_device_ids=true | all-gather | bytes 176256 | tf_op jit(solution)/shard_map/all_gather | solution.py:54
  45.9 0.8 compare_select_fusion.2
  47.0 19.7 %gather_fusion.3 = f32[10112,81]{1,0:T(8,128)} fusion(f32[81,513]{0,1:T(8,128)S(1)} %concatenate.21, s32[10240]{0:T(1024)S(1)} %pad_clamp_fusion.1), kind=kCustom, calls=%fused_computation.3 | custom fusion | bytes 6593024 | tf_op jit(solution)/shard_map/gather | solution.py:59
  66.7 6.0 %copy.79 = f32[316,32,81]{0,1,2:T(8,128)} copy(f32[316,32,81]{2,1,0:T(8,128)} %bitcast.78) | data formatting | bytes 6552576 | tf_op jit(solution)/shard_map/gather | solution.py:59
  73.0 8.3 %fusion.26 = bf16[32,81,1]{1,0,2:T(8,128)(2,1)S(1)} fusion(bf16[316,81,81]{0,2,1:T(8,128)(2,1)} %param.14, f32[316,32,81]{0,1,2:T(8,128)} %copy.79), kind=kOutput, calls=%fused_computation.23 | convolution fusion | flops 796140544 | bytes 7428024 | tf_op jit(solution)/shard_map/okc,cob->kb/dot_general | solution.py:56
  82.5 69.3 %while.11 = (s32[]{:T(128)}, f32[256,16]{0,1:T(8,128)S(1)}, s32[27,256]{1,0:T(8,128)}, f32[4,289,16]{2,0,1:T(4,128)S(1)}, f32[4,256,16]{1,2,0:T(8,128)S(1)}, /*index=5*/s32[]{:T(128)}, s32[]{:T(128)}) while((s32[]{:T(128)}, f32[256,16]{0,1:T(8,128)S(1)}, s32[27,256]{1,0:T(8,128)}, f32[4,289,16]{2,0,1:T(4,128)S(1)}, ...), condition=%wide.region_2.3_spmd.clone, body=%wide.region_0.2_spmd.clone.sunk | while | flops 726787 | bytes 680027 | solution.py:37
  82.5 0.7 compare_select_fusion.5
  83.3 1.0 gather_fusion
  85.1 0.7 compare_select_fusion.5
  85.8 1.0 gather_fusion
  87.7 0.7 compare_select_fusion.5
  88.4 1.0 gather_fusion
  90.2 0.7 compare_select_fusion.5
  91.0 1.0 gather_fusion
  92.8 0.7 compare_select_fusion.5
  93.5 1.0 gather_fusion
  95.4 0.7 compare_select_fusion.5
  96.1 1.0 gather_fusion
  98.7 1.0 gather_fusion
  101.2 1.0 gather_fusion
  103.1 0.7 compare_select_fusion.5
  103.8 1.0 gather_fusion
  106.4 1.0 gather_fusion
  108.9 1.0 gather_fusion
  110.8 0.7 compare_select_fusion.5
  111.5 1.0 gather_fusion
  114.1 1.0 gather_fusion
  115.9 0.7 compare_select_fusion.5
  116.6 1.0 gather_fusion
  119.2 1.0 gather_fusion
  121.8 1.0 gather_fusion
  123.6 0.7 compare_select_fusion.5
  124.3 1.0 gather_fusion
  126.9 1.0 gather_fusion
  128.7 0.7 compare_select_fusion.5
  129.5 1.0 gather_fusion
  131.3 0.7 compare_select_fusion.5
  132.0 1.0 gather_fusion
  134.6 1.0 gather_fusion
  137.2 1.0 gather_fusion
  139.7 1.0 gather_fusion
  141.6 0.7 compare_select_fusion.5
  142.3 1.0 gather_fusion
  144.1 0.7 compare_select_fusion.5
  144.9 1.0 gather_fusion
  147.4 1.0 gather_fusion
  149.3 0.7 compare_select_fusion.5
  150.0 1.0 gather_fusion
  152.0 0.7 reshape.137
  152.8 282.6 %gather_fusion.2 = bf16[80896,81]{1,0:T(8,128)(2,1)} fusion(bf16[81,769]{0,1:T(8,128)(2,1)S(1)} %maximum_maximum_fusion, s32[80896]{0:T(1024)S(1)} %broadcast_clamp_fusion), kind=kCustom, calls=%fused_computation.2 | custom fusion | bytes 26533888 | tf_op jit(solution)/shard_map/gather | solution.py:50
  435.4 25.3 %copy.73 = bf16[316,256,81]{1,0,2:T(8,128)(2,1)} copy(bf16[316,256,81]{2,1,0:T(8,128)(2,1)} %bitcast.79) | data formatting | bytes 26210304 | tf_op jit(solution)/shard_map/gather | solution.py:50
  460.7 9.0 %fusion.11 = f32[81,256]{1,0:T(8,128)} fusion(f32[81,256]{1,0:T(8,128)S(1)} %copy.83, bf16[316,81,81]{0,2,1:T(8,128)(2,1)} %param.14, bf16[316,256,81]{1,0,2:T(8,128)(2,1)} %copy.73), kind=kOutput, calls=%fused_computation.19 | convolution fusion | flops 1061538048 | bytes 17417592 | tf_op jit(solution)/shard_map/okc,cob->kb/dot_general | solution.py:49
  (291 shorter events, 33.5 us)
Async XLA Ops:
  0.6 80.6 %copy-start = (bf16[8,81,81]{2,0,1:T(8,128)(2,1)S(1)}, bf16[8,81,81]{2,0,1:T(8,128)(2,1)}, u32[]{:S(2)}) copy-start(bf16[8,81,81]{2,0,1:T(8,128)(2,1)} %param.16) | copy-start | bytes 314932
  4.3 148.4 %all-to-all-start = ((bf16[81,16,32]{0,2,1:T(8,128)(2,1)}), bf16[81,16,32]{0,2,1:T(8,128)(2,1)S(1)}, u32[]{:S(2)}, u32[]{:S(2)}) async-start(bf16[81,16,32]{0,2,1:T(8,128)(2,1)} %bitcast.2), calls=%async_computation | async-start | bytes 262144 | tf_op jit(solution)/shard_map/all_to_all | solution.py:45
  14.0 67.7 %collective-permute-start = (f32[4,256]{1,0:T(4,128)S(1)}, f32[4,256]{1,0:T(4,128)S(1)}, u32[]{:S(2)}, u32[]{:S(2)}) collective-permute-start(f32[4,256]{1,0:T(4,128)S(1)} %get-tuple-element.80), channel_id=1, source_target_pairs={{0,1},{1,2},{2,3},{3,4},{4,5},{5,6},{6,7},{7,8},{8,9},{9,10},{10,1... | collective-permute-start | bytes 12296 | tf_op jit(solution)/shard_map/ppermute | solution.py:18
  17.5 64.2 %collective-permute-start.1 = (f32[4,256]{1,0:T(4,128)S(1)}, f32[4,256]{1,0:T(4,128)S(1)}, u32[]{:S(2)}, u32[]{:S(2)}) collective-permute-start(f32[4,256]{1,0:T(4,128)S(1)} %get-tuple-element.81), channel_id=1, source_target_pairs={{1,0},{2,1},{3,2},{4,3},{5,4},{6,5},{7,6},{8,7},{9,8},{10,9},{11,1... | collective-permute-start | bytes 12296 | tf_op jit(solution)/shard_map/ppermute | solution.py:21
  66.7 6.1 %copy-start.2 = (s32[256]{0:T(256)S(1)}, s32[256]{0:T(256)}, u32[]{:S(2)}) copy-start(s32[256]{0:T(256)} %param.22) | copy-start | bytes 3076
  72.8 9.0 %copy-start.1 = (f32[3,4096]{1,0:T(4,128)S(1)}, f32[3,4096]{1,0:T(4,128)}, u32[]{:S(2)}) copy-start(f32[3,4096]{1,0:T(4,128)} %param.20) | copy-start | bytes 147460
where the time goes:
time: 472 us; the launch traced here: 470 us
  local copies, waits for them, and re-layouts  386 us (82%)
  other arithmetic  27.8 us (6%)
  blocking collectives  22.5 us (5%)
  matrix products  18.5 us (4%)
  starting transfers between devices  12.8 us (3%)
    gather x2, local copies, waits for them, and re-layouts, far_part(): sources[:, leaf_lists]  308 us
    gather x27, local copies, waits for them, and re-layouts, step(): source = extended[:, index, :]  26.9 us
    gather x2, local copies, waits for them, and re-layouts, far_part(): parent_ext[:, coarse_lists]  25.7 us
    all_gather x1, blocking collectives, far_part(): lax.all_gather(parents, ('dom', 'slab', 'half'), axis=1, tiled=True)  22.5 us
    select_n x27, other arithmetic, step(): source = extended[:, index, :]  19.1 us
    slice x27, local copies, waits for them, and re-layouts, step(): source[3][:, None, :] * lax.rsqrt(dist + softening)  10.2 us
  transfers between devices with their start and end apart: 3, of which 0 were waited for; matrix products, arithmetic and copies ran while one was open for 24% of the time, Pallas kernels for 0%

commit v1 on v0

v1 whole, which is shorter than its diff:
```python
import functools

import jax
import jax.numpy as jnp
from jax import lax
from jax.experimental import pallas as pl
from jax.experimental.pallas import tpu as pltpu
from jax.sharding import PartitionSpec as P

HALO = 16
CAP = 32
LANES = 128
WIDE = 256
ROWS = 88
STEP = 8

softening = 0.01
DEVICES = ("dom", "slab", "half")
f32 = jnp.float32
bf16 = jnp.bfloat16


def one_hot(row, width):
    picks = lax.broadcasted_iota(jnp.int32, (width, row.shape[1]), 0) == row
    return jnp.where(picks, 1.0, 0.0).astype(bf16)


def pick_block(stacked, block, first, stride, count):
    value = jnp.zeros((ROWS, stacked.shape[1]), f32)
    for j in range(count):
        start = first + j * stride
        value = jnp.where(block == j, stacked[start : start + ROWS], value)
    return value


def far_kernel(
    leaf_ref, arrived_ref, translate_ref, down_ref, lists_ref, clists_ref, out_ref,
    source_ref, parent_ref, matrix_ref, column_ref, acc_ref,
):
    coeffs, boxes = leaf_ref.shape
    offsets = translate_ref.shape[0]
    peers = arrived_ref.shape[0]
    together = WIDE // CAP
    groups = peers // together
    matrix_ref[...] = jnp.zeros_like(matrix_ref)
    acc_ref[...] = jnp.zeros_like(acc_ref)

    def turned(j, kind):
        part = arrived_ref[j * together : (j + 1) * together, kind * CAP : (kind + 1) * CAP, :]
        return jnp.transpose(part.reshape(WIDE, LANES).astype(f32))[:ROWS]

    own = jnp.concatenate([leaf_ref[...].astype(f32), jnp.zeros((ROWS - coeffs, boxes), f32)], 0)
    source_ref[...] = jnp.concatenate([own] + [turned(j, 0) for j in range(groups)], 0).astype(bf16)
    parent_ref[...] = jnp.concatenate(
        [turned(j, kind) for j in range(groups) for kind in (1, 2)], 0
    ).astype(bf16)
    lane_group = lax.broadcasted_iota(jnp.int32, (1, WIDE), 1) // (WIDE // STEP)
    fill = jnp.zeros((LANES - ROWS, WIDE), f32)

    def step(s, carry):
        row = clists_ref[s]
        rows = lists_ref[pl.ds(pl.multiple_of(s * STEP, STEP), STEP), :]
        found = jnp.dot(parent_ref[...], one_hot(row % WIDE, WIDE), preferred_element_type=f32)
        high = pick_block(found, row // WIDE, 0, 2 * ROWS, groups)
        low = pick_block(found, row // WIDE, ROWS, 2 * ROWS, groups)
        low = jnp.concatenate([low[:, LANES:], low[:, :LANES]], 1)
        for i in range(STEP):
            offset = s * STEP + i
            row = rows[i : i + 1]
            found = jnp.dot(source_ref[...], one_hot(row % WIDE, WIDE), preferred_element_type=f32)
            column = pick_block(found, row // WIDE, 0, ROWS, groups + 1)
            column_ref[LANES * i : LANES * (i + 1), :WIDE] = jnp.concatenate([column, fill], 0).astype(bf16)
            column = jnp.where(
                lane_group == i, high, jnp.where(lane_group == (i + STEP // 2) % STEP, low, 0.0)
            )
            column_ref[LANES * i : LANES * (i + 1), WIDE:] = jnp.concatenate([column, fill], 0).astype(bf16)
            matrix_ref[:coeffs, LANES * i : LANES * i + coeffs] = translate_ref[
                jnp.minimum(offset, offsets - 1)
            ]
        acc_ref[...] += jnp.dot(matrix_ref[...], column_ref[...], preferred_element_type=f32)
        return carry

    lax.fori_loop(0, clists_ref.shape[0], step, 0)
    coarse = acc_ref[:, WIDE : WIDE + LANES] + acc_ref[:, WIDE + LANES :]
    coarse = coarse + pltpu.roll(coarse, LANES // 2, 1)
    coarse = coarse + pltpu.roll(coarse, LANES // 4, 1)
    coarse_round = coarse.astype(bf16)
    box = lax.broadcasted_iota(jnp.int32, (LANES, boxes), 1)
    parent = lax.broadcasted_iota(jnp.int32, (LANES, boxes), 0)
    spread = jnp.dot(
        coarse_round, jnp.where(box // 8 == parent, 1.0, 0.0).astype(bf16), preferred_element_type=f32
    )[:coeffs]
    octant = lax.broadcasted_iota(jnp.int32, (1, boxes), 1) % 8
    total = acc_ref[:coeffs, :WIDE]
    for c in range(8):
        total = total + jnp.dot(
            down_ref[c], jnp.where(octant == c, spread, 0.0).astype(bf16), preferred_element_type=f32
        )
    out_ref[...] = total


def far_sum(leaf_multipoles, arrived, translate, shift_down, leaf_lists, coarse_lists):
    coeffs, boxes = leaf_multipoles.shape
    offsets, coarse = coarse_lists.shape
    assert boxes == WIDE and coarse * STEP == WIDE
    peers = arrived.shape[0]
    groups = peers * CAP // WIDE
    steps = -(-offsets // STEP)
    extra = ((0, steps * STEP - offsets), (0, 0))
    lists = jnp.pad(leaf_lists, extra, constant_values=boxes + peers * CAP)
    clists = jnp.pad(coarse_lists, extra, constant_values=peers * coarse).reshape(steps, 1, WIDE)
    return pl.pallas_call(
        far_kernel,
        out_shape=jax.ShapeDtypeStruct((coeffs, boxes), f32),
        in_specs=[pl.BlockSpec(memory_space=pltpu.VMEM)] * 6,
        out_specs=pl.BlockSpec(memory_space=pltpu.VMEM),
        scratch_shapes=[
            pltpu.VMEM(((groups + 1) * ROWS, WIDE), bf16),
            pltpu.VMEM((groups * 2 * ROWS, WIDE), bf16),
            pltpu.VMEM((ROWS, STEP * LANES), bf16),
            pltpu.VMEM((STEP * LANES, 2 * WIDE), bf16),
            pltpu.VMEM((ROWS, 2 * WIDE), f32),
        ],
        compiler_params=pltpu.CompilerParams(vmem_limit_bytes=40 * 2**20),
        name="far",
    )(leaf_multipoles, arrived, translate, shift_down, lists, clists)


def near_kernel(atoms_ref, edges_ref, lists_ref, counts_ref, out_ref):
    slots, boxes = out_ref.shape
    tiles = boxes // LANES

    def tile_sum(t):
        lanes = slice(t * LANES, (t + 1) * LANES)
        target = [atoms_ref[k * slots : (k + 1) * slots, lanes] for k in range(3)]

        def step(n, total):
            entry = lists_ref[n, :, lanes]
            local = entry - HALO
            inside = jnp.broadcast_to(local // LANES == t, (8, LANES)) & jnp.broadcast_to(local >= 0, (8, LANES))
            first = jnp.broadcast_to(local & (LANES - 1), (8, LANES))
            second = jnp.broadcast_to(local & (2 * HALO - 1), (8, LANES))
            source = []
            for r in range(4 * slots // 8):
                rows = slice(8 * r, 8 * (r + 1))
                one = jnp.take_along_axis(atoms_ref[rows, lanes], first, axis=1)
                two = jnp.take_along_axis(edges_ref[rows, lanes], second, axis=1)
                source.append(jnp.where(inside, one, two))
            source = jnp.concatenate(source, 0)
            present = entry < boxes + 2 * HALO
            charge = jnp.where(present, source[3 * slots :], 0.0)
            for b in range(slots):
                square = jnp.full((slots, LANES), softening, f32)
                for k in range(3):
                    diff = target[k] - source[k * slots + b : k * slots + b + 1]
                    square = square + diff * diff
                total = total + charge[b : b + 1] * lax.rsqrt(square)
            return total

        return lax.fori_loop(0, lists_ref.shape[0], step, jnp.zeros((slots, LANES), f32))

    slot = lax.broadcasted_iota(jnp.int32, (slots, LANES), 0)
    for t in range(tiles):
        lanes = slice(t * LANES, (t + 1) * LANES)
        out_ref[:, lanes] = jnp.where(slot < counts_ref[:, lanes], tile_sum(t), 0.0)


def near_part(positions, charges, counts, near_lists):
    boxes = counts.shape[0]
    slots = charges.shape[0] // boxes
    valid = jnp.arange(slots, dtype=jnp.int32)[:, None] < counts[None, :]
    charge = jnp.where(valid, charges.reshape(boxes, slots).T, 0.0)
    place = positions.reshape(3, boxes, slots).transpose(0, 2, 1).reshape(3 * slots, boxes)
    atoms = jnp.concatenate([place, charge], 0)
    count = lax.axis_size(DEVICES)
    forward = [(i, i + 1) for i in range(count - 1)]
    backward = [(target, source) for source, target in forward]
    below = lax.ppermute(atoms[:, boxes - HALO :], DEVICES, forward)
    above = lax.ppermute(atoms[:, :HALO], DEVICES, backward)
    fill = jnp.zeros((4 * slots, LANES - 2 * HALO), f32)
    edges = []
    for t in range(boxes // LANES):
        low, high = t * LANES, (t + 1) * LANES
        edges += [
            atoms[:, high : high + HALO] if high < boxes else above,
            atoms[:, low - HALO : low] if t else below,
            fill,
        ]
    potential = pl.pallas_call(
        near_kernel,
        out_shape=jax.ShapeDtypeStruct((slots, boxes), f32),
        in_specs=[pl.BlockSpec(memory_space=pltpu.VMEM)] * 4,
        out_specs=pl.BlockSpec(memory_space=pltpu.VMEM),
        name="near",
        cost_estimate=pl.CostEstimate(flops=40_000_000, bytes_accessed=2**18, transcendentals=0),
    )(atoms, jnp.concatenate(edges, 1), near_lists[:, None, :], counts[None, :])
    return potential.T.reshape(boxes * slots)


def far_part(leaf_multipoles, translate, shift_up, shift_down, export_rows, leaf_lists, coarse_lists):
    coeffs, boxes = leaf_multipoles.shape
    peers = export_rows.shape[1]
    exported = leaf_multipoles[:, export_rows[0].reshape(-1)].T.reshape(peers, CAP, coeffs)
    children = leaf_multipoles.reshape(coeffs, boxes // 8, 8)
    parents = jnp.einsum("ckm,mpc->pk", shift_up, children, preferred_element_type=f32)
    high = lax.reduce_precision(parents, 8, 7)
    both = jnp.concatenate([high, parents - high], 0).astype(bf16)
    outgoing = jnp.concatenate(
        [exported, jnp.broadcast_to(both[None], (peers,) + both.shape)], 1
    )
    outgoing = jnp.pad(outgoing, ((0, 0), (0, 0), (0, LANES - coeffs)))
    arrived = lax.all_to_all(outgoing, DEVICES, split_axis=0, concat_axis=0, tiled=True)
    return far_sum(leaf_multipoles, arrived, translate, shift_down, leaf_lists, coarse_lists)


def body(
    leaf_multipoles, translate, shift_up, shift_down, export_rows, leaf_lists, coarse_lists,
    positions, charges, counts, near_lists,
):
    local_field = far_part(
        leaf_multipoles, translate, shift_up, shift_down, export_rows, leaf_lists, coarse_lists
    )
    near_potential = near_part(positions, charges, counts, near_lists)
    return (local_field, near_potential)


def solution(mesh):
    every = ("rep",) + DEVICES
    in_specs = (
        P(None, every), P(), P(), P(), P(every, None, None), P(None, every), P(None, every),
        P(None, every), P(every), P(every), P(None, every),
    )
    out_specs = (P(None, every), P(every))
    return jax.shard_map(body, mesh=mesh, in_specs=in_specs, out_specs=out_specs, check_vma=False)
```

time: 472 us -> 84.2 us (0.18)
  local copies, waits for them, and re-layouts: 386 us -> 24.7 us
  Pallas kernels: 0 us -> 42.4 us
  other arithmetic: 27.8 us -> 2.39 us
  blocking collectives: 22.5 us -> 0 us
  matrix products: 18.5 us -> 0.16 us
    gather x32 -> x1, local copies, waits for them, and re-layouts: 362 us -> 1.34 us  [far_part(): leaf_multipoles[:, export_rows[0].reshape(-1)].T.reshape(peers, CAP, coeffs)]
    pallas_call x0 -> x2, Pallas kernels: none -> 42.4 us  [the longest x1 33 us: far_sum(): pl.pallas_call(far_kernel, out_shape=jax.ShapeDtypeStruct((coeffs, boxes)...]
    all_gather x1 -> x0, blocking collectives: 22.5 us -> none  [far_part(): lax.all_gather(parents, ('dom', 'slab', 'half'), axis=1, tiled=True)]
    select_n x30 -> x2, other arithmetic: 20.9 us -> 0.75 us  [the longest x1 0.74 us: near_part(): charge = jnp.where(valid, charges.reshape(boxes, slots).T, 0.0)]
    dot_general x4 -> x1, matrix products: 18.5 us -> 0.16 us  [far_part(): jnp.einsum('ckm,mpc->pk', shift_up, children, preferred_element_type=f32)]
    unnamed x8 -> x12, local copies, waits for them, and re-layouts: 1.35 us -> 16.7 us
    slice x27 -> x0, local copies, waits for them, and re-layouts: 10.2 us -> none  [step(): source[3][:, None, :] * lax.rsqrt(dist + softening)]
    sub x108 -> x0, local copies, waits for them, and re-layouts: 5.57 us -> none  [step(): diff = targets[axis_id][:, :, None] - source[axis_id][:, None, :]]
  transfers between devices with their start and end apart: 3 -> 3, of which waited for: 0 -> 0; matrix products, arithmetic and copies ran while one was open for 24% -> 24% of each run, Pallas kernels for 0% -> 11%
where the time goes in v1:
time: 84.2 us; the launch traced here: 83.2 us
  Pallas kernels  42.4 us (50%)
  local copies, waits for them, and re-layouts  24.7 us (29%)
  starting transfers between devices  12.8 us (15%)
  other arithmetic  2.39 us (3%)
    pallas_call x1, Pallas kernels, far_sum(): pl.pallas_call(far_kernel, out_shape=jax.ShapeDtypeStruct((coeffs, boxes)...  33 us
    unnamed x12, local copies, waits for them, and re-layouts  16.7 us
    pallas_call x1, Pallas kernels, near_part(): pl.pallas_call(near_kernel, out_shape=jax.ShapeDtypeStruct((slots, boxes)...  9.41 us
    all_to_all x1, starting transfers between devices, far_part(): lax.all_to_all(outgoing, DEVICES, split_axis=0, concat_axis=0, tiled=True)  7.32 us
    ppermute x1, starting transfers between devices, near_part(): below = lax.ppermute(atoms[:, boxes - HALO:], DEVICES, forward)  3.54 us
    ppermute x1, starting transfers between devices, near_part(): above = lax.ppermute(atoms[:, :HALO], DEVICES, backward)  1.92 us
  transfers between devices with their start and end apart: 3, of which 0 were waited for; matrix products, arithmetic and copies ran while one was open for 24% of the time, Pallas kernels for 11%

profile of v1, /device:TPU:1, one launch (start us, length us, event | category | flops | bytes accessed | tf_op | source)
XLA Modules:
  0.0 83.2 jit_solution(10780560876686958177)
XLA Ops:
  0.6 0.0 copy-start
  0.6 0.8 reshape_squeeze.3
  1.5 0.9 %copy.20 = bf16[81,256]{0,1:T(8,128)(2,1)S(1)} copy(bf16[81,256]{1,0:T(8,128)(2,1)} %leaf_ref.1) | data formatting | bytes 82944 | tf_op args[0]
  2.4 1.3 %gather_fusion = bf16[512,81]{1,0:T(8,128)(2,1)S(1)} fusion(bf16[81,256]{0,1:T(8,128)(2,1)S(1)} %copy.20, s32[1024]{0:T(1024)S(1)} %pad_clamp_fusion), kind=kCustom, calls=%fused_computation | custom fusion | bytes 167936 | tf_op jit(solution)/shard_map/gather | solution.py:203
  3.7 0.0 copy-done
  3.7 0.2 reduce-precision_convert_fusion
  4.0 0.9 %fusion.2 = bf16[16,96,128]{2,1,0:T(8,128)(2,1)} fusion(bf16[16,64,81]{2,1,0:T(8,128)(2,1)S(1)} %broadcast_in_dim.22, bf16[16,32,81]{2,1,0:T(8,128)(2,1)S(1)} %bitcast.15), kind=kLoop, calls=%fused_computation.5 | loop fusion | flops 1376256 | bytes 642048 | tf_op jit(solution)/shard_map/concatenate | solution.py:208
  4.9 7.3 %all-to-all-start = ((bf16[16,96,128]{2,1,0:T(8,128)(2,1)}), bf16[16,96,128]{2,1,0:T(8,128)(2,1)S(1)}, u32[]{:S(2)}, u32[]{:S(2)}) async-start(bf16[16,96,128]{2,1,0:T(8,128)(2,1)} %fusion.2), calls=%async_computation | async-start | bytes 786432 | tf_op jit(solution)/shard_map/all_to_all | solution.py:212
  12.2 0.8 reshape.74
  13.0 0.1 copy.29
  13.1 1.0 %reshape.72 = f32[3,256,16]{2,1,0:T(8,128)S(1)} reshape(f32[3,4096]{1,0:T(4,128)} %param.18) | data formatting | bytes 98304 | tf_op jit(solution)/shard_map/reshape | solution.py:173
  14.1 0.1 copy.28
  14.2 0.0 copy-start.3
  14.2 0.7 bitcast_select_fusion
  15.0 0.1 fusion.8
  15.1 3.5 %collective-permute-start = (f32[64,16]{1,0:T(8,128)S(1)}, f32[64,16]{1,0:T(8,128)S(1)}, u32[]{:S(2)}, u32[]{:S(2)}) collective-permute-start(f32[64,16]{1,0:T(8,128)S(1)} %get-tuple-element.4), channel_id=1, source_target_pairs={{0,1},{1,2},{2,3},{3,4},{4,5},{5,6},{6,7},{7,8},{8,9},{9,10},{10,1... | collective-permute-start | bytes 12296 | tf_op jit(solution)/shard_map/ppermute | solution.py:178
  18.6 1.9 %collective-permute-start.1 = (f32[64,16]{1,0:T(8,128)S(1)}, f32[64,16]{1,0:T(8,128)S(1)}, u32[]{:S(2)}, u32[]{:S(2)}) collective-permute-start(f32[64,16]{1,0:T(8,128)S(1)} %get-tuple-element.5), channel_id=1, source_target_pairs={{1,0},{2,1},{3,2},{4,3},{5,4},{6,5},{7,6},{8,7},{9,8},{10,9},{11,1... | collective-permute-start | bytes 12296 | tf_op jit(solution)/shard_map/ppermute | solution.py:179
  20.5 0.6 pad_maximum_fusion.atoms_ref
  21.2 1.4 %broadcast_in_dim.25.lists_ref = s32[27,1,256]{2,1,0:T(1,128)} reshape(s32[27,256]{1,0:T(8,128)} %param.21) | data formatting | bytes 55296 | tf_op jit(solution)/shard_map/broadcast_in_dim | solution.py:196
  22.6 0.9 %copy.31 = s32[316,32]{1,0:T(8,128)S(1)} copy(s32[316,32]{0,1:T(8,128)} %param.17) | data formatting | bytes 80896
  23.5 0.1 reshape.85.clists_ref
  23.6 0.0 copy-start.2
  23.6 1.0 %copy.26.down_ref = bf16[8,81,81]{2,1,0:T(8,128)(2,1)S(1)} copy(bf16[8,81,81]{2,0,1:T(8,128)(2,1)} %param.14) | data formatting | bytes 209952 | tf_op args[3]
  24.6 10.8 %copy.25.translate_ref = bf16[316,81,81]{2,1,0:T(8,128)(2,1)} copy(bf16[316,81,81]{0,2,1:T(8,128)(2,1)} %param.12) | data formatting | bytes 8293104 | tf_op args[1]
  35.4 0.0 copy-done.3
  35.5 0.0 collective-permute-done
  35.5 0.0 collective-permute-done.1
  35.5 0.7 concatenate.20.edges_ref
  36.2 9.4 %near.1 = f32[16,256]{1,0:T(8,128)} custom-call(f32[64,256]{1,0:T(8,128)} %pad_maximum_fusion.atoms_ref, f32[64,256]{1,0:T(8,128)} %concatenate.20.edges_ref, s32[27,1,256]{2,1,0:T(1,128)} %broadcast_in_dim.25.lists_ref, s32[1,256]{1,0:T(1,128)} %bitcast.18), custom_call_target="tpu_custom_call" | custom-call | flops 40000000 | bytes 262144 | tf_op jit(solution)/shard_map/near/pallas_call | solution.py:189
  45.6 0.8 copy.30
  46.5 0.7 reshape.75
  47.2 0.0 all-to-all-done.arrived_ref
  47.2 0.0 copy-done.2
  47.2 0.0 copy-start.1
  47.2 3.0 %copy-done.1 = bf16[316,81,81]{2,1,0:T(8,128)(2,1)S(1)} copy-done((bf16[316,81,81]{2,1,0:T(8,128)(2,1)S(1)}, bf16[316,81,81]{2,1,0:T(8,128)(2,1)}, u32[]{:S(2)}) %copy-start.1) | copy-done | bytes 4146576
  50.2 33.0 %far.1 = f32[81,256]{1,0:T(8,128)} custom-call(bf16[81,256]{1,0:T(8,128)(2,1)S(1)} %copy-done.2, bf16[16,96,128]{2,1,0:T(8,128)(2,1)S(1)} %all-to-all-done.arrived_ref, bf16[316,81,81]{2,1,0:T(8,128)(2,1)S(1)} %copy-done.1, bf16[8,81,81]{2,1,0:T(8,128)(2,1)S(1)} %copy.26.down_ref, s32[320,256]{1,0:T(8,128)S(1)} %pad.13.lists_ref, ...), custom_call_target="tpu_custom_call" | custom-call | tf_op jit(solution)/shard_map/far/pallas_call | solution.py:112
  (7 shorter events, 0.1 us)
Async XLA Ops:
  0.6 3.1 %copy-start = (bf16[8,81,81]{2,0,1:T(8,128)(2,1)S(1)}, bf16[8,81,81]{2,0,1:T(8,128)(2,1)}, u32[]{:S(2)}) copy-start(bf16[8,81,81]{2,0,1:T(8,128)(2,1)} %param.13) | copy-start | bytes 314932
  4.9 42.3 %all-to-all-start = ((bf16[16,96,128]{2,1,0:T(8,128)(2,1)}), bf16[16,96,128]{2,1,0:T(8,128)(2,1)S(1)}, u32[]{:S(2)}, u32[]{:S(2)}) async-start(bf16[16,96,128]{2,1,0:T(8,128)(2,1)} %fusion.2), calls=%async_computation | async-start | bytes 786432 | tf_op jit(solution)/shard_map/all_to_all | solution.py:212
  14.2 21.2 %copy-start.3 = (s32[316,256]{1,0:T(8,128)S(1)}, s32[316,256]{1,0:T(8,128)}, u32[]{:S(2)}) copy-start(s32[316,256]{1,0:T(8,128)} %param.16) | copy-start | bytes 970756
  15.1 20.4 %collective-permute-start = (f32[64,16]{1,0:T(8,128)S(1)}, f32[64,16]{1,0:T(8,128)S(1)}, u32[]{:S(2)}, u32[]{:S(2)}) collective-permute-start(f32[64,16]{1,0:T(8,128)S(1)} %get-tuple-element.4), channel_id=1, source_target_pairs={{0,1},{1,2},{2,3},{3,4},{4,5},{5,6},{6,7},{7,8},{8,9},{9,10},{10,1... | collective-permute-start | bytes 12296 | tf_op jit(solution)/shard_map/ppermute | solution.py:178
  18.6 16.9 %collective-permute-start.1 = (f32[64,16]{1,0:T(8,128)S(1)}, f32[64,16]{1,0:T(8,128)S(1)}, u32[]{:S(2)}, u32[]{:S(2)}) collective-permute-start(f32[64,16]{1,0:T(8,128)S(1)} %get-tuple-element.5), channel_id=1, source_target_pairs={{1,0},{2,1},{3,2},{4,3},{5,4},{6,5},{7,6},{8,7},{9,8},{10,9},{11,1... | collective-permute-start | bytes 12296 | tf_op jit(solution)/shard_map/ppermute | solution.py:179
  23.6 23.6 %copy-start.2 = (bf16[81,256]{1,0:T(8,128)(2,1)S(1)}, bf16[81,256]{1,0:T(8,128)(2,1)}, u32[]{:S(2)}) copy-start(bf16[81,256]{1,0:T(8,128)(2,1)} %leaf_ref.1) | copy-start | bytes 124420
  47.2 3.0 %copy-start.1 = (bf16[316,81,81]{2,1,0:T(8,128)(2,1)S(1)}, bf16[316,81,81]{2,1,0:T(8,128)(2,1)}, u32[]{:S(2)}) copy-start(bf16[316,81,81]{2,1,0:T(8,128)(2,1)} %copy.25.translate_ref) | copy-start | bytes 12439660

commit v2 on v1

--- a/solution.py
+++ b/solution.py
@@ -21,8 +21,9 @@
 
 
 def one_hot(row, width):
-    picks = lax.broadcasted_iota(jnp.int32, (width, row.shape[1]), 0) == row
-    return jnp.where(picks, 1.0, 0.0).astype(bf16)
+    numbers = lax.broadcasted_iota(jnp.int32, (width, row.shape[1]), 0).astype(f32).astype(bf16)
+    picks = numbers == row.astype(f32).astype(bf16)
+    return jnp.where(picks, jnp.ones((), bf16), jnp.zeros((), bf16))
 
 
 def pick_block(stacked, block, first, stride, count):
@@ -38,11 +39,19 @@
     source_ref, parent_ref, matrix_ref, column_ref, acc_ref,
 ):
     coeffs, boxes = leaf_ref.shape
-    offsets = translate_ref.shape[0]
+    offsets = translate_ref.shape[2]
     peers = arrived_ref.shape[0]
     together = WIDE // CAP
     groups = peers // together
-    matrix_ref[...] = jnp.zeros_like(matrix_ref)
+
+    def turn(k, carry):
+        rows = jnp.concatenate(
+            [translate_ref[k].astype(f32), jnp.zeros((LANES - coeffs, offsets), f32)], 0
+        )
+        matrix_ref[pl.ds(k, offsets, stride=ROWS), :] = jnp.transpose(rows)
+        return carry
+
+    lax.fori_loop(0, coeffs, turn, 0, unroll=9)
     acc_ref[...] = jnp.zeros_like(acc_ref)
 
     def turned(j, kind):
@@ -55,6 +64,7 @@
         [turned(j, kind) for j in range(groups) for kind in (1, 2)], 0
     ).astype(bf16)
     lane_group = lax.broadcasted_iota(jnp.int32, (1, WIDE), 1) // (WIDE // STEP)
+    mine = [jnp.where(lane_group == i, 1.0, 0.0).astype(bf16) for i in range(STEP)]
     fill = jnp.zeros((LANES - ROWS, WIDE), f32)
 
     def step(s, carry):
@@ -64,23 +74,25 @@
         high = pick_block(found, row // WIDE, 0, 2 * ROWS, groups)
         low = pick_block(found, row // WIDE, ROWS, 2 * ROWS, groups)
         low = jnp.concatenate([low[:, LANES:], low[:, :LANES]], 1)
+        high = jnp.concatenate([high, fill], 0).astype(bf16)
+        low = jnp.concatenate([low, fill], 0).astype(bf16)
+        matrix = []
         for i in range(STEP):
             offset = s * STEP + i
             row = rows[i : i + 1]
             found = jnp.dot(source_ref[...], one_hot(row % WIDE, WIDE), preferred_element_type=f32)
             column = pick_block(found, row // WIDE, 0, ROWS, groups + 1)
             column_ref[LANES * i : LANES * (i + 1), :WIDE] = jnp.concatenate([column, fill], 0).astype(bf16)
-            column = jnp.where(
-                lane_group == i, high, jnp.where(lane_group == (i + STEP // 2) % STEP, low, 0.0)
+            column_ref[LANES * i : LANES * (i + 1), WIDE:] = (
+                high * mine[i] + low * mine[(i + STEP // 2) % STEP]
             )
-            column_ref[LANES * i : LANES * (i + 1), WIDE:] = jnp.concatenate([column, fill], 0).astype(bf16)
-            matrix_ref[:coeffs, LANES * i : LANES * i + coeffs] = translate_ref[
-                jnp.minimum(offset, offsets - 1)
-            ]
-        acc_ref[...] += jnp.dot(matrix_ref[...], column_ref[...], preferred_element_type=f32)
+            start = pl.multiple_of(jnp.minimum(offset, offsets - 1) * ROWS, ROWS)
+            matrix.append(matrix_ref[pl.ds(start, ROWS), :].astype(bf16))
+        matrix = jnp.concatenate(matrix, 1)
+        acc_ref[...] += jnp.dot(matrix, column_ref[...], preferred_element_type=f32)
         return carry
 
-    lax.fori_loop(0, clists_ref.shape[0], step, 0)
+    lax.fori_loop(0, clists_ref.shape[0], step, 0, unroll=2)
     coarse = acc_ref[:, WIDE : WIDE + LANES] + acc_ref[:, WIDE + LANES :]
     coarse = coarse + pltpu.roll(coarse, LANES // 2, 1)
     coarse = coarse + pltpu.roll(coarse, LANES // 4, 1)
@@ -117,13 +129,13 @@
         scratch_shapes=[
             pltpu.VMEM(((groups + 1) * ROWS, WIDE), bf16),
             pltpu.VMEM((groups * 2 * ROWS, WIDE), bf16),
-            pltpu.VMEM((ROWS, STEP * LANES), bf16),
+            pltpu.VMEM((offsets * ROWS, LANES), f32),
             pltpu.VMEM((STEP * LANES, 2 * WIDE), bf16),
             pltpu.VMEM((ROWS, 2 * WIDE), f32),
         ],
         compiler_params=pltpu.CompilerParams(vmem_limit_bytes=40 * 2**20),
         name="far",
-    )(leaf_multipoles, arrived, translate, shift_down, lists, clists)
+    )(leaf_multipoles, arrived, translate.transpose(1, 2, 0), shift_down, lists, clists)
 
 
 def near_kernel(atoms_ref, edges_ref, lists_ref, counts_ref, out_ref):

time: 84.2 us -> 68.7 us (0.82)
  local copies, waits for them, and re-layouts: 24.7 us -> 12.5 us
  Pallas kernels: 42.4 us -> 39 us
    unnamed x12 -> x13, local copies, waits for them, and re-layouts: 16.7 us -> 4.48 us
    pallas_call x1, Pallas kernels: 33 us -> 29.6 us  [far_sum(): pl.pallas_call(far_kernel, out_shape=jax.ShapeDtypeStruct((coeffs, boxes)...]
  transfers between devices with their start and end apart: 3 -> 3, of which waited for: 0 -> 1; matrix products, arithmetic and copies ran while one was open for 24% -> 12% of each run, Pallas kernels for 11% -> 14%
where the time goes in v2:
time: 68.7 us; the launch traced here: 68 us
  Pallas kernels  39 us (57%)
  starting transfers between devices  12.8 us (19%)
  local copies, waits for them, and re-layouts  12.5 us (18%)
  other arithmetic  2.33 us (3%)
  between operations  0.8 us (1%)
    pallas_call x1, Pallas kernels, far_sum(): pl.pallas_call(far_kernel, out_shape=jax.ShapeDtypeStruct((coeffs, boxes)...  29.6 us
    pallas_call x1, Pallas kernels, near_part(): pl.pallas_call(near_kernel, out_shape=jax.ShapeDtypeStruct((slots, boxes)...  9.42 us
    all_to_all x1, starting transfers between devices, far_part(): lax.all_to_all(outgoing, DEVICES, split_axis=0, concat_axis=0, tiled=True)  7.32 us
    unnamed x13, local copies, waits for them, and re-layouts  4.48 us
    ppermute x1, starting transfers between devices, near_part(): below = lax.ppermute(atoms[:, boxes - HALO:], DEVICES, forward)  3.54 us
    ppermute x1, starting transfers between devices, near_part(): above = lax.ppermute(atoms[:, :HALO], DEVICES, backward)  1.92 us
    broadcast_in_dim x1, local copies, waits for them, and re-layouts, near_part(): near_lists[:, None, :]  1.39 us
  transfers between devices with their start and end apart: 3, of which 1 were waited for; matrix products, arithmetic and copies ran while one was open for 12% of the time, Pallas kernels for 14%

profile of v2, /device:TPU:1, one launch (start us, length us, event | category | flops | bytes accessed | tf_op | source)
XLA Modules:
  0.0 68.0 jit_solution(13133988434203758493)
XLA Ops:
  0.6 0.0 copy-start
  0.6 0.0 copy-start.2
  0.7 0.0 copy-start.4
  0.7 0.0 copy-start.3
  0.7 1.0 %copy.19 = bf16[81,256]{0,1:T(8,128)(2,1)S(1)} copy(bf16[81,256]{1,0:T(8,128)(2,1)} %leaf_ref.1) | data formatting | bytes 82944 | tf_op args[0]
  1.6 0.8 %reshape_squeeze.3 = s32[512,1]{0,1:T(1,128)S(1)} reshape(s32[1,16,32]{2,1,0:T(8,128)} %param.15) | data formatting | bytes 4096 | tf_op jit(solution)/shard_map/reshape;squeeze | solution.py:215
  2.4 1.3 %gather_fusion = bf16[512,81]{1,0:T(8,128)(2,1)S(1)} fusion(bf16[81,256]{0,1:T(8,128)(2,1)S(1)} %copy.19, s32[1024]{0:T(1024)S(1)} %pad_clamp_fusion), kind=kCustom, calls=%fused_computation | custom fusion | bytes 167936 | tf_op jit(solution)/shard_map/gather | solution.py:215
  3.8 0.0 copy-done
  3.8 0.2 reduce-precision_convert_fusion
  4.0 0.9 %fusion.2 = bf16[16,96,128]{2,1,0:T(8,128)(2,1)} fusion(bf16[16,64,81]{2,1,0:T(8,128)(2,1)S(1)} %broadcast_in_dim.22, bf16[16,32,81]{2,1,0:T(8,128)(2,1)S(1)} %bitcast.17), kind=kLoop, calls=%fused_computation.5 | loop fusion | flops 1376256 | bytes 642048 | tf_op jit(solution)/shard_map/concatenate | solution.py:220
  4.9 7.3 %all-to-all-start = ((bf16[16,96,128]{2,1,0:T(8,128)(2,1)}), bf16[16,96,128]{2,1,0:T(8,128)(2,1)S(1)}, u32[]{:S(2)}, u32[]{:S(2)}) async-start(bf16[16,96,128]{2,1,0:T(8,128)(2,1)} %fusion.2), calls=%async_computation | async-start | bytes 786432 | tf_op jit(solution)/shard_map/all_to_all | solution.py:224
  12.2 1.0 %reshape.72 = f32[3,256,16]{2,1,0:T(8,128)S(1)} reshape(f32[3,4096]{1,0:T(4,128)} %param.18) | data formatting | bytes 98304 | tf_op jit(solution)/shard_map/reshape | solution.py:185
  13.3 0.1 copy.26
  13.4 0.8 %reshape.74 = f32[256,16]{1,0:T(8,128)S(1)} reshape(f32[4096]{0:T(1024)} %param.19) | data formatting | bytes 32768 | tf_op jit(solution)/shard_map/reshape | solution.py:184
  14.2 0.1 copy.27
  14.3 0.7 %bitcast_select_fusion = f32[16,256]{1,0:T(8,128)S(1)} fusion(f32[256,16]{0,1:T(8,128)S(1)} %copy.27, s32[256]{0:T(256)} %param.20), kind=kLoop, calls=%fused_computation.25 | loop fusion | flops 8192 | bytes 33792 | tf_op jit(solution)/shard_map/jit(_where)/select_n | solution.py:184
  15.0 0.1 fusion.8
  15.0 3.5 %collective-permute-start = (f32[64,16]{1,0:T(8,128)S(1)}, f32[64,16]{1,0:T(8,128)S(1)}, u32[]{:S(2)}, u32[]{:S(2)}) collective-permute-start(f32[64,16]{1,0:T(8,128)S(1)} %get-tuple-element.4), channel_id=1, source_target_pairs={{0,1},{1,2},{2,3},{3,4},{4,5},{5,6},{6,7},{7,8},{8,9},{9,10},{10,1... | collective-permute-start | bytes 12296 | tf_op jit(solution)/shard_map/ppermute | solution.py:190
  18.6 1.9 %collective-permute-start.1 = (f32[64,16]{1,0:T(8,128)S(1)}, f32[64,16]{1,0:T(8,128)S(1)}, u32[]{:S(2)}, u32[]{:S(2)}) collective-permute-start(f32[64,16]{1,0:T(8,128)S(1)} %get-tuple-element.5), channel_id=1, source_target_pairs={{1,0},{2,1},{3,2},{4,3},{5,4},{6,5},{7,6},{8,7},{9,8},{10,9},{11,1... | collective-permute-start | bytes 12296 | tf_op jit(solution)/shard_map/ppermute | solution.py:191
  20.5 0.6 pad_maximum_fusion.atoms_ref
  21.2 1.4 %broadcast_in_dim.25.lists_ref = s32[27,1,256]{2,1,0:T(1,128)} reshape(s32[27,256]{1,0:T(8,128)} %param.21) | data formatting | bytes 55296 | tf_op jit(solution)/shard_map/broadcast_in_dim | solution.py:208
  22.5 0.9 %copy.29 = s32[316,32]{1,0:T(8,128)S(1)} copy(s32[316,32]{0,1:T(8,128)} %param.17) | data formatting | bytes 80896
  23.5 0.1 reshape.85.clists_ref
  23.6 0.0 copy-done.4
  23.7 0.0 copy-done.3
  23.7 0.0 collective-permute-done
  23.7 0.5 collective-permute-done.1
  24.2 0.7 %concatenate.20.edges_ref = f32[64,256]{1,0:T(8,128)} concatenate(f32[64,16]{1,0:T(8,128)S(1)} %get-tuple-element.3, f32[64,16]{1,0:T(8,128)S(1)} %collective-permute-done, f32[64,96]{1,0:T(8,128)S(1)} %broadcast_in_dim.24, f32[64,16]{1,0:T(8,128)S(1)} %collective-permute-done.1, f32[64,16]{1,0:T(8,128)S(1)} %get-tuple-element.2, f32[64,96]{1,0:T(8,128)S(1)} %broadcast_in_dim.24), dimensions={1} | concatenate | bytes 131072 | tf_op jit(solution)/shard_map/concatenate | solution.py:208
  24.9 9.4 %near.1 = f32[16,256]{1,0:T(8,128)} custom-call(f32[64,256]{1,0:T(8,128)} %pad_maximum_fusion.atoms_ref, f32[64,256]{1,0:T(8,128)} %concatenate.20.edges_ref, s32[27,1,256]{2,1,0:T(1,128)} %broadcast_in_dim.25.lists_ref, s32[1,256]{1,0:T(1,128)} %bitcast.20), custom_call_target="tpu_custom_call" | custom-call | flops 40000000 | bytes 262144 | tf_op jit(solution)/shard_map/near/pallas_call | solution.py:201
  34.3 0.8 %copy.28 = f32[256,16]{1,0:T(8,128)S(1)} copy(f32[256,16]{0,1:T(8,128)} %bitcast.18) | data formatting | bytes 32768 | tf_op jit(solution)/shard_map/transpose | solution.py:209
  35.1 0.7 %reshape.75 = f32[4096]{0:T(1024)} reshape(f32[256,16]{1,0:T(8,128)S(1)} %copy.28) | data formatting | bytes 32768 | tf_op jit(solution)/shard_map/reshape | solution.py:209
  35.8 0.0 all-to-all-done.arrived_ref
  35.8 0.0 copy-done.2
  35.8 0.0 copy-start.1
  35.8 2.6 %copy-done.1 = bf16[316,81,81]{0,2,1:T(8,128)(2,1)S(1)} copy-done((bf16[316,81,81]{0,2,1:T(8,128)(2,1)S(1)}, bf16[316,81,81]{0,2,1:T(8,128)(2,1)}, u32[]{:S(2)}) %copy-start.1) | copy-done | bytes 4146576
  38.4 29.6 %far.1 = f32[81,256]{1,0:T(8,128)} custom-call(bf16[81,256]{1,0:T(8,128)(2,1)S(1)} %copy-done.2, bf16[16,96,128]{2,1,0:T(8,128)(2,1)S(1)} %all-to-all-done.arrived_ref, bf16[81,81,316]{2,1,0:T(8,128)(2,1)S(1)} %bitcast.12, bf16[8,81,81]{2,1,0:T(8,128)(2,1)S(1)} %copy.24.down_ref, s32[320,256]{1,0:T(8,128)S(1)} %pad.13.lists_ref, ...), custom_call_target="tpu_custom_call" | custom-call | tf_op jit(solution)/shard_map/far/pallas_call | solution.py:124
  (8 shorter events, 0.2 us)
Async XLA Ops:
  0.6 3.2 %copy-start = (bf16[8,81,81]{2,0,1:T(8,128)(2,1)S(1)}, bf16[8,81,81]{2,0,1:T(8,128)(2,1)}, u32[]{:S(2)}) copy-start(bf16[8,81,81]{2,0,1:T(8,128)(2,1)} %param.13) | copy-start | bytes 314932
  0.6 35.2 %copy-start.2 = (bf16[81,256]{1,0:T(8,128)(2,1)S(1)}, bf16[81,256]{1,0:T(8,128)(2,1)}, u32[]{:S(2)}) copy-start(bf16[81,256]{1,0:T(8,128)(2,1)} %leaf_ref.1) | copy-start | bytes 124420
  0.7 23.0 %copy-start.4 = (bf16[8,81,81]{2,0,1:T(8,128)(2,1)S(1)}, bf16[8,81,81]{2,0,1:T(8,128)(2,1)}, u32[]{:S(2)}) copy-start(bf16[8,81,81]{2,0,1:T(8,128)(2,1)} %param.14) | copy-start | bytes 314932
  0.7 23.0 %copy-start.3 = (s32[316,256]{1,0:T(8,128)S(1)}, s32[316,256]{1,0:T(8,128)}, u32[]{:S(2)}) copy-start(s32[316,256]{1,0:T(8,128)} %param.16) | copy-start | bytes 970756
  4.9 30.9 %all-to-all-start = ((bf16[16,96,128]{2,1,0:T(8,128)(2,1)}), bf16[16,96,128]{2,1,0:T(8,128)(2,1)S(1)}, u32[]{:S(2)}, u32[]{:S(2)}) async-start(bf16[16,96,128]{2,1,0:T(8,128)(2,1)} %fusion.2), calls=%async_computation | async-start | bytes 786432 | tf_op jit(solution)/shard_map/all_to_all | solution.py:224
  15.0 8.7 %collective-permute-start = (f32[64,16]{1,0:T(8,128)S(1)}, f32[64,16]{1,0:T(8,128)S(1)}, u32[]{:S(2)}, u32[]{:S(2)}) collective-permute-start(f32[64,16]{1,0:T(8,128)S(1)} %get-tuple-element.4), channel_id=1, source_target_pairs={{0,1},{1,2},{2,3},{3,4},{4,5},{5,6},{6,7},{7,8},{8,9},{9,10},{10,1... | collective-permute-start | bytes 12296 | tf_op jit(solution)/shard_map/ppermute | solution.py:190
  18.6 5.6 %collective-permute-start.1 = (f32[64,16]{1,0:T(8,128)S(1)}, f32[64,16]{1,0:T(8,128)S(1)}, u32[]{:S(2)}, u32[]{:S(2)}) collective-permute-start(f32[64,16]{1,0:T(8,128)S(1)} %get-tuple-element.5), channel_id=1, source_target_pairs={{1,0},{2,1},{3,2},{4,3},{5,4},{6,5},{7,6},{8,7},{9,8},{10,9},{11,1... | collective-permute-start | bytes 12296 | tf_op jit(solution)/shard_map/ppermute | solution.py:191
  35.8 2.6 %copy-start.1 = (bf16[316,81,81]{0,2,1:T(8,128)(2,1)S(1)}, bf16[316,81,81]{0,2,1:T(8,128)(2,1)}, u32[]{:S(2)}) copy-start(bf16[316,81,81]{0,2,1:T(8,128)(2,1)} %param.12) | copy-start | bytes 12439660

commit v3 on v2

v3 whole, which is shorter than its diff:
```python
import jax
import jax.numpy as jnp
from jax import lax
from jax.experimental import pallas as pl
from jax.experimental.pallas import tpu as pltpu
from jax.sharding import PartitionSpec as P

HALO = 16
CAP = 32
LANES = 128
WIDE = 256
ROWS = 88
STEP = 8

softening = 0.01
DEVICES = ("dom", "slab", "half")
f32 = jnp.float32
bf16 = jnp.bfloat16


def one_hot(row, width):
    numbers = lax.broadcasted_iota(jnp.int32, (width, row.shape[1]), 0).astype(f32).astype(bf16)
    picks = numbers == row.astype(f32).astype(bf16)
    return jnp.where(picks, jnp.ones((), bf16), jnp.zeros((), bf16))


def pick_block(stacked, block, first, stride, count):
    value = jnp.zeros((ROWS, stacked.shape[1]), f32)
    for j in range(count):
        start = first + j * stride
        value = jnp.where(block == j, stacked[start : start + ROWS], value)
    return value


def far_kernel(
    source_ref, parent_ref, translate_ref, down_ref, lists_ref, clists_ref, out_ref,
    page_ref, matrix_ref, column_ref, acc_ref, page_sem,
):
    coeffs, boxes = out_ref.shape
    offsets = translate_ref.shape[2]
    pieces = page_sem.shape[0]
    pages = coeffs // pieces
    groups = source_ref.shape[0] // ROWS - 1

    def fetch(j):
        part = pl.ds(j * pages, pages)
        return pltpu.make_async_copy(translate_ref.at[part], page_ref.at[part], page_sem.at[j])

    for j in range(pieces):
        fetch(j).start()
    acc_ref[...] = jnp.zeros_like(acc_ref)

    def turn(j, carry):
        fetch(j).wait()
        for i in range(pages):
            k = j * pages + i
            rows = jnp.concatenate(
                [page_ref[k].astype(f32), jnp.zeros((LANES - coeffs, offsets), f32)], 0
            )
            matrix_ref[pl.ds(k, offsets, stride=ROWS), :] = jnp.transpose(rows)
        return carry

    lax.fori_loop(0, pieces, turn, 0)
    lane_group = lax.broadcasted_iota(jnp.int32, (1, WIDE), 1) // (WIDE // STEP)
    mine = [jnp.where(lane_group == i, 1.0, 0.0).astype(bf16) for i in range(STEP)]
    fill = jnp.zeros((LANES - ROWS, WIDE), f32)

    def step(s, carry):
        row = clists_ref[s]
        rows = lists_ref[pl.ds(pl.multiple_of(s * STEP, STEP), STEP), :]
        found = jnp.dot(parent_ref[...], one_hot(row % WIDE, WIDE), preferred_element_type=f32)
        high = pick_block(found, row // WIDE, 0, 2 * ROWS, groups)
        low = pick_block(found, row // WIDE, ROWS, 2 * ROWS, groups)
        low = jnp.concatenate([low[:, LANES:], low[:, :LANES]], 1)
        high = jnp.concatenate([high, fill], 0).astype(bf16)
        low = jnp.concatenate([low, fill], 0).astype(bf16)
        matrix = []
        for i in range(STEP):
            offset = s * STEP + i
            row = rows[i : i + 1]
            found = jnp.dot(source_ref[...], one_hot(row % WIDE, WIDE), preferred_element_type=f32)
            column = pick_block(found, row // WIDE, 0, ROWS, groups + 1)
            column_ref[LANES * i : LANES * (i + 1), :WIDE] = jnp.concatenate([column, fill], 0).astype(bf16)
            column_ref[LANES * i : LANES * (i + 1), WIDE:] = (
                high * mine[i] + low * mine[(i + STEP // 2) % STEP]
            )
            start = pl.multiple_of(jnp.minimum(offset, offsets - 1) * ROWS, ROWS)
            matrix.append(matrix_ref[pl.ds(start, ROWS), :].astype(bf16))
        matrix = jnp.concatenate(matrix, 1)
        acc_ref[...] += jnp.dot(matrix, column_ref[...], preferred_element_type=f32)
        return carry

    lax.fori_loop(0, clists_ref.shape[0], step, 0, unroll=2)
    coarse = acc_ref[:, WIDE : WIDE + LANES] + acc_ref[:, WIDE + LANES :]
    coarse = coarse + pltpu.roll(coarse, LANES // 2, 1)
    coarse = coarse + pltpu.roll(coarse, LANES // 4, 1)
    coarse_round = coarse.astype(bf16)
    box = lax.broadcasted_iota(jnp.int32, (LANES, boxes), 1)
    parent = lax.broadcasted_iota(jnp.int32, (LANES, boxes), 0)
    spread = jnp.dot(
        coarse_round, jnp.where(box // 8 == parent, 1.0, 0.0).astype(bf16), preferred_element_type=f32
    )[:coeffs]
    octant = lax.broadcasted_iota(jnp.int32, (1, boxes), 1) % 8
    total = acc_ref[:coeffs, :WIDE]
    for c in range(8):
        total = total + jnp.dot(
            down_ref[c], jnp.where(octant == c, spread, 0.0).astype(bf16), preferred_element_type=f32
        )
    out_ref[...] = total


def far_sum(source, parents, translate, shift_down, leaf_lists, coarse_lists):
    offsets, boxes = leaf_lists.shape
    coeffs = translate.shape[1]
    coarse = coarse_lists.shape[1]
    assert boxes == WIDE and coarse * STEP == WIDE
    groups = source.shape[0] // ROWS - 1
    steps = -(-offsets // STEP)
    extra = ((0, steps * STEP - offsets), (0, 0))
    lists = jnp.pad(leaf_lists, extra, constant_values=(groups + 1) * WIDE)
    clists = jnp.pad(coarse_lists, extra, constant_values=groups * WIDE).reshape(steps, 1, WIDE)
    vmem = pl.BlockSpec(memory_space=pltpu.VMEM)
    return pl.pallas_call(
        far_kernel,
        out_shape=jax.ShapeDtypeStruct((coeffs, boxes), f32),
        in_specs=[vmem, vmem, pl.BlockSpec(memory_space=pl.ANY), vmem, vmem, vmem],
        out_specs=vmem,
        scratch_shapes=[
            pltpu.VMEM((coeffs, coeffs, offsets), bf16),
            pltpu.VMEM((offsets * ROWS, LANES), f32),
            pltpu.VMEM((STEP * LANES, 2 * WIDE), bf16),
            pltpu.VMEM((ROWS, 2 * WIDE), f32),
            pltpu.SemaphoreType.DMA((9 if coeffs % 9 == 0 else 1,)),
        ],
        compiler_params=pltpu.CompilerParams(vmem_limit_bytes=48 * 2**20),
        name="far",
    )(source, parents, translate.transpose(1, 2, 0), shift_down, lists, clists)


def exchange_kernel(
    leaf_ref, rows_ref, up_ref, atoms_ref, lists_ref, counts_ref,
    source_ref, parent_ref, near_ref,
    send_ref, land_ref, edge_ref, side_ref, send_sem, land_sem, edge_send_sem, edge_land_sem,
):
    coeffs, boxes = leaf_ref.shape
    slots = near_ref.shape[0]
    peers = send_ref.shape[0]
    tiles = boxes // LANES
    sizes = [lax.axis_size(axis) for axis in DEVICES]
    dom, slab, half = [lax.axis_index(axis) for axis in DEVICES]
    me = (dom * sizes[1] + slab) * sizes[2] + half

    def place(index):
        return {
            "dom": index // (sizes[1] * sizes[2]),
            "slab": (index // sizes[2]) % sizes[1],
            "half": index % sizes[2],
        }

    barrier = pltpu.get_barrier_semaphore()

    def greet(d, carry):
        pl.semaphore_signal(
            barrier, inc=1, device_id=place((me + d) % peers), device_id_type=pl.DeviceIdType.MESH
        )
        return carry

    lax.fori_loop(1, peers, greet, 0)

    own = jnp.concatenate([leaf_ref[...].astype(f32), jnp.zeros((LANES - coeffs, boxes), f32)], 0)
    packed = own.astype(bf16)
    up = up_ref[...]
    high = up.astype(bf16)
    low = (up - high.astype(f32)).astype(bf16)
    together = WIDE // CAP
    for j in range(peers // together):
        hot = one_hot(rows_ref[:, j * WIDE : (j + 1) * WIDE], boxes)
        part = jnp.transpose(jnp.dot(packed, hot, preferred_element_type=f32)).astype(bf16)
        for i in range(together):
            p = j * together + i
            send_ref[p, :CAP, :] = part[i * CAP : (i + 1) * CAP]
            send_ref[p, CAP : 2 * CAP, :] = high
            send_ref[p, 2 * CAP :, :] = low
    pl.semaphore_wait(barrier, peers - 1)

    def edge(side):
        lanes = pl.ds((1 - side) * (boxes - LANES), LANES)
        return pltpu.make_async_remote_copy(
            src_ref=atoms_ref.at[:, lanes], dst_ref=edge_ref.at[side],
            send_sem=edge_send_sem.at[side], recv_sem=edge_land_sem.at[side],
            device_id=place((me + 1 - 2 * side + peers) % peers),
            device_id_type=pl.DeviceIdType.MESH,
        )

    def sending(d):
        return pltpu.make_async_remote_copy(
            src_ref=send_ref.at[(me + d) % peers], dst_ref=land_ref.at[me],
            send_sem=send_sem.at[d], recv_sem=land_sem.at[d],
            device_id=place((me + d) % peers), device_id_type=pl.DeviceIdType.MESH,
        )

    def landing(d):
        sender = (me - d + peers) % peers
        return pltpu.make_async_remote_copy(
            src_ref=send_ref.at[sender], dst_ref=land_ref.at[sender],
            send_sem=send_sem.at[d], recv_sem=land_sem.at[d],
            device_id=place(sender), device_id_type=pl.DeviceIdType.MESH,
        )

    for side in range(2):
        edge(side).start()

    def start(d, carry):
        sending(d).start()
        return carry

    lax.fori_loop(1, peers, start, 0)
    land_ref[me] = send_ref[me]

    for side in range(2):
        edge(side).wait()
    below = jnp.where(me > 0, edge_ref[0], 0.0)
    above = jnp.where(me < peers - 1, edge_ref[1], 0.0)
    lower = lax.broadcasted_iota(jnp.int32, (1, LANES), 1) < LANES // 2
    for t in range(tiles):
        after = atoms_ref[:, (t + 1) * LANES : (t + 2) * LANES] if t + 1 < tiles else above
        before = atoms_ref[:, (t - 1) * LANES : t * LANES] if t else below
        side_ref[:, t * LANES : (t + 1) * LANES] = jnp.where(lower, after, before)

    def step(n, totals):
        out = []
        for t in range(tiles):
            lanes = slice(t * LANES, (t + 1) * LANES)
            total = totals[t]
            entry = lists_ref[n, :, lanes]
            local = jnp.broadcast_to(entry - HALO, (8, LANES))
            inside = (local >= t * LANES) & (local < (t + 1) * LANES)
            lane = local & (LANES - 1)
            source = []
            for r in range(4 * slots // 8):
                rows = slice(8 * r, 8 * (r + 1))
                one = jnp.take_along_axis(atoms_ref[rows, lanes], lane, axis=1)
                two = jnp.take_along_axis(side_ref[rows, lanes], lane, axis=1)
                source.append(jnp.where(inside, one, two))
            source = jnp.concatenate(source, 0)
            charge = jnp.where(entry < boxes + 2 * HALO, source[3 * slots :], 0.0)
            target = [atoms_ref[k * slots : (k + 1) * slots, lanes] for k in range(3)]
            for b in range(slots):
                square = jnp.full((slots, LANES), softening, f32)
                for k in range(3):
                    diff = target[k] - source[k * slots + b : k * slots + b + 1]
                    square = square + diff * diff
                total = total + charge[b : b + 1] * lax.rsqrt(square)
            out.append(total)
        return tuple(out)

    zero = jnp.zeros((slots, LANES), f32)
    totals = lax.fori_loop(0, lists_ref.shape[0], step, (zero,) * tiles)
    slot = lax.broadcasted_iota(jnp.int32, (slots, LANES), 0)
    for t in range(tiles):
        lanes = slice(t * LANES, (t + 1) * LANES)
        near_ref[:, lanes] = jnp.where(slot < counts_ref[:, lanes], totals[t], 0.0)

    def finish(d, carry):
        sending(d).wait_send()
        landing(d).wait_recv()
        return carry

    lax.fori_loop(1, peers, finish, 0)

    def turned(j, kind):
        part = land_ref[j * together : (j + 1) * together, kind * CAP : (kind + 1) * CAP, :]
        return jnp.transpose(part.reshape(WIDE, LANES).astype(f32))[:ROWS]

    groups = peers // together
    source_ref[...] = jnp.concatenate(
        [own[:ROWS]] + [turned(j, 0) for j in range(groups)], 0
    ).astype(bf16)
    parent_ref[...] = jnp.concatenate(
        [turned(j, kind) for j in range(groups) for kind in (1, 2)], 0
    ).astype(bf16)


def exchange(leaf_multipoles, shift_up, export_rows, positions, charges, counts, near_lists):
    coeffs, boxes = leaf_multipoles.shape
    peers = export_rows.shape[1]
    slots = charges.shape[0] // boxes
    groups = peers * CAP // WIDE
    assert boxes // 8 == CAP
    children = leaf_multipoles.reshape(coeffs, boxes // 8, 8)
    parents = jnp.einsum("ckm,mpc->pk", shift_up, children, preferred_element_type=f32)
    parents = jnp.pad(parents, ((0, 0), (0, LANES - coeffs)))
    valid = jnp.arange(slots, dtype=jnp.int32)[:, None] < counts[None, :]
    charge = jnp.where(valid, charges.reshape(boxes, slots).T, 0.0)
    place = positions.reshape(3, boxes, slots).transpose(0, 2, 1).reshape(3 * slots, boxes)
    atoms = jnp.concatenate([place, charge], 0)
    vmem = pl.BlockSpec(memory_space=pltpu.VMEM)
    source, parent, potential = pl.pallas_call(
        exchange_kernel,
        out_shape=(
            jax.ShapeDtypeStruct(((groups + 1) * ROWS, WIDE), bf16),
            jax.ShapeDtypeStruct((groups * 2 * ROWS, WIDE), bf16),
            jax.ShapeDtypeStruct((slots, boxes), f32),
        ),
        in_specs=[vmem] * 6,
        out_specs=(vmem,) * 3,
        scratch_shapes=[
            pltpu.VMEM((peers, 3 * CAP, LANES), bf16),
            pltpu.VMEM((peers, 3 * CAP, LANES), bf16),
            pltpu.VMEM((2, 4 * slots, LANES), f32),
            pltpu.VMEM((4 * slots, boxes), f32),
            pltpu.SemaphoreType.DMA((peers,)),
            pltpu.SemaphoreType.DMA((peers,)),
            pltpu.SemaphoreType.DMA((2,)),
            pltpu.SemaphoreType.DMA((2,)),
        ],
        compiler_params=pltpu.CompilerParams(
            collective_id=0, has_side_effects=True, vmem_limit_bytes=32 * 2**20
        ),
        name="exchange",
    )(
        leaf_multipoles, export_rows.reshape(1, peers * CAP), parents, atoms,
        near_lists[:, None, :], counts[None, :],
    )
    return source, parent, potential.T.reshape(boxes * slots)


def body(
    leaf_multipoles, translate, shift_up, shift_down, export_rows, leaf_lists, coarse_lists,
    positions, charges, counts, near_lists,
):
    source, parents, near_potential = exchange(
        leaf_multipoles, shift_up, export_rows, positions, charges, counts, near_lists
    )
    local_field = far_sum(source, parents, translate, shift_down, leaf_lists, coarse_lists)
    return (local_field, near_potential)


def solution(mesh):
    every = ("rep",) + DEVICES
    in_specs = (
        P(None, every), P(), P(), P(), P(every, None, None), P(None, every), P(None, every),
        P(None, every), P(every), P(every), P(None, every),
    )
    out_specs = (P(None, every), P(every))
    return jax.shard_map(body, mesh=mesh, in_specs=in_specs, out_specs=out_specs, check_vma=False)
```

time: 68.7 us -> 58.8 us (0.86)
  starting transfers between devices: 12.8 us -> 0 us
  Pallas kernels: 39 us -> 46.5 us
  local copies, waits for them, and re-layouts: 12.5 us -> 9.81 us
  other arithmetic: 2.33 us -> 0.7 us
    all_to_all x1 -> x0, starting transfers between devices: 7.32 us -> none  [far_part(): lax.all_to_all(outgoing, DEVICES, split_axis=0, concat_axis=0, tiled=True)]
    pallas_call x1, Pallas kernels: 9.42 us -> 15.8 us  [exchange(): pl.pallas_call(exchange_kernel, out_shape=(jax.ShapeDtypeStruct(((groups...]
    ppermute x2 -> x0, starting transfers between devices: 5.46 us -> none  [the longest x1 3.54 us: near_part(): below = lax.ppermute(atoms[:, boxes - HALO:], DEVICES, forward)]
    concatenate x4 -> x1, other arithmetic: 1.61 us -> 0.01 us  [exchange(): atoms = jnp.concatenate([place, charge], 0)]
    gather x1 -> x0, local copies, waits for them, and re-layouts: 1.34 us -> none  [far_part(): leaf_multipoles[:, export_rows[0].reshape(-1)].T.reshape(peers, CAP, coeffs)]
    pallas_call x1, Pallas kernels: 29.6 us -> 30.7 us  [far_sum(): pl.pallas_call(far_kernel, out_shape=jax.ShapeDtypeStruct((coeffs, boxes)...]
    pad x2 -> x3, local copies, waits for them, and re-layouts: 0.04 us -> 1.03 us  [the longest x1 1 us: far_sum(): lists = jnp.pad(leaf_lists, extra, constant_values=(groups + 1) * WIDE)]
    reshape x5 -> x6, local copies, waits for them, and re-layouts: 2.71 us -> 3.53 us  [the longest x1 1.04 us: exchange(): positions.reshape(3, boxes, slots).transpose(0, 2, 1)]
  transfers between devices with their start and end apart: 3 -> 0, of which waited for: 1 -> 0; matrix products, arithmetic and copies ran while one was open for 12% -> 0% of each run, Pallas kernels for 14% -> 0%
where the time goes in v3:
time: 58.8 us; the launch traced here: 57.9 us
  Pallas kernels  46.5 us (79%)
  local copies, waits for them, and re-layouts  9.81 us (17%)
  between operations  0.72 us (1%)
  other arithmetic  0.7 us (1%)
    pallas_call x1, Pallas kernels, far_sum(): pl.pallas_call(far_kernel, out_shape=jax.ShapeDtypeStruct((coeffs, boxes)...  30.7 us
    pallas_call x1, Pallas kernels, exchange(): pl.pallas_call(exchange_kernel, out_shape=(jax.ShapeDtypeStruct(((groups...  15.8 us
    unnamed x9, local copies, waits for them, and re-layouts  4.24 us

profile of v3, /device:TPU:1, one launch (start us, length us, event | category | flops | bytes accessed | tf_op | source)
XLA Modules:
  0.0 57.9 jit_solution(15218408357504573829)
XLA Ops:
  0.6 0.0 copy-start
  0.6 1.0 %reshape.28 = f32[3,256,16]{2,1,0:T(8,128)S(1)} reshape(f32[3,4096]{1,0:T(4,128)} %param.18) | data formatting | bytes 98304 | tf_op jit(solution)/shard_map/reshape | solution.py:295
  1.7 0.1 copy.21
  1.8 0.8 %reshape.30 = f32[256,16]{1,0:T(8,128)S(1)} reshape(f32[4096]{0:T(1024)} %param.19) | data formatting | bytes 32768 | tf_op jit(solution)/shard_map/reshape | solution.py:294
  2.6 0.1 copy.22
  2.7 0.7 %bitcast_select_fusion = f32[16,256]{1,0:T(8,128)S(1)} fusion(f32[256,16]{0,1:T(8,128)S(1)} %copy.22, s32[256]{0:T(256)} %param.20), kind=kLoop, calls=%fused_computation.4 | loop fusion | flops 8192 | bytes 33792 | tf_op jit(solution)/shard_map/jit(_where)/select_n | solution.py:294
  3.4 0.9 %copy.18 = bf16[81,256]{0,1:T(8,128)(2,1)S(1)} copy(bf16[81,256]{1,0:T(8,128)(2,1)} %leaf_ref.1) | data formatting | bytes 82944 | tf_op args[0]
  4.3 0.0 copy-done
  4.3 0.2 convolution_bitcast_fusion
  4.5 0.8 %broadcast_in_dim.13.lists_ref = s32[27,1,256]{2,1,0:T(1,128)S(1)} reshape(s32[27,256]{1,0:T(8,128)} %param.21) | data formatting | bytes 55296 | tf_op jit(solution)/shard_map/broadcast_in_dim | solution.py:323
  5.3 0.8 %reshape.26.rows_ref = s32[1,512]{1,0:T(1,128)S(1)} reshape(s32[1,16,32]{2,1,0:T(8,128)} %param.15) | data formatting | bytes 4096 | tf_op jit(solution)/shard_map/reshape | solution.py:322
  6.1 0.0 copy-start.1
  6.1 0.8 %copy-done.1 = bf16[81,256]{1,0:T(8,128)(2,1)S(1)} copy-done((bf16[81,256]{1,0:T(8,128)(2,1)S(1)}, bf16[81,256]{1,0:T(8,128)(2,1)}, u32[]{:S(2)}) %copy-start.1) | copy-done | bytes 41496
  6.9 0.0 copy-start.2
  6.9 0.7 %copy-done.2 = s32[256]{0:T(256)S(1)} copy-done((s32[256]{0:T(256)S(1)}, s32[256]{0:T(256)}, u32[]{:S(2)}) %copy-start.2) | copy-done | bytes 1048
  7.6 15.8 %exchange.1 = (bf16[264,256]{1,0:T(8,128)(2,1)S(1)}, bf16[352,256]{1,0:T(8,128)(2,1)S(1)}, f32[16,256]{1,0:T(8,128)S(1)}) custom-call(bf16[81,256]{1,0:T(8,128)(2,1)S(1)} %copy-done.1, s32[1,512]{1,0:T(1,128)S(1)} %reshape.26.rows_ref, f32[32,128]{1,0:T(8,128)S(1)} %pad.12.up_ref, f32[64,256]{1,0:T(8,128)S(1)} %pad_maximum_fusion.atoms_ref, ...), custom_call_target="tpu_custom_call" | custom-call | tf_op jit(solution)/shard_map/exchange/pallas_call | solution.py:298
  23.4 0.9 %copy.27 = s32[316,32]{1,0:T(8,128)S(1)} copy(s32[316,32]{0,1:T(8,128)} %param.17) | data formatting | bytes 80896
  24.3 0.1 reshape.34.clists_ref
  24.4 1.0 %pad.13.lists_ref = s32[320,256]{1,0:T(8,128)S(1)} pad(s32[316,256]{1,0:T(8,128)} %param.16, s32[]{:T(128)} %constant.1.clone.1), padding=0_4x0_0 | pad | bytes 651268 | tf_op jit(solution)/shard_map/jit(_pad)/pad | solution.py:120
  25.4 0.9 %copy.24.down_ref = bf16[8,81,81]{2,1,0:T(8,128)(2,1)S(1)} copy(bf16[8,81,81]{2,0,1:T(8,128)(2,1)} %param.14) | data formatting | bytes 209952 | tf_op args[3]
  26.4 30.7 %far.1 = f32[81,256]{1,0:T(8,128)} custom-call(bf16[264,256]{1,0:T(8,128)(2,1)S(1)} %get-tuple-element.5.source_ref, bf16[352,256]{1,0:T(8,128)(2,1)S(1)} %get-tuple-element.6.parent_ref, bf16[81,81,316]{2,1,0:T(8,128)(2,1)} %bitcast.12, bf16[8,81,81]{2,1,0:T(8,128)(2,1)S(1)} %copy.24.down_ref, s32[320,256]{1,0:T(8,128)S(1)} %pad.13.lists_ref, ...), custom_call_target="tpu_custom_call" | custom-call | tf_op jit(solution)/shard_map/far/pallas_call | solution.py:123
  57.1 0.1 copy.26
  57.2 0.7 %reshape.32 = f32[4096]{0:T(1024)} reshape(f32[256,16]{1,0:T(8,128)S(1)} %copy.26) | data formatting | bytes 32768 | tf_op jit(solution)/shard_map/reshape | solution.py:325
  (3 shorter events, 0.0 us)
Async XLA Ops:
  0.6 3.7 %copy-start = (bf16[8,81,81]{2,0,1:T(8,128)(2,1)S(1)}, bf16[8,81,81]{2,0,1:T(8,128)(2,1)}, u32[]{:S(2)}) copy-start(bf16[8,81,81]{2,0,1:T(8,128)(2,1)} %param.13) | copy-start | bytes 314932
  6.1 0.8 %copy-start.1 = (bf16[81,256]{1,0:T(8,128)(2,1)S(1)}, bf16[81,256]{1,0:T(8,128)(2,1)}, u32[]{:S(2)}) copy-start(bf16[81,256]{1,0:T(8,128)(2,1)} %leaf_ref.1) | copy-start | bytes 124420
  6.9 0.7 %copy-start.2 = (s32[256]{0:T(256)S(1)}, s32[256]{0:T(256)}, u32[]{:S(2)}) copy-start(s32[256]{0:T(256)} %param.20) | copy-start | bytes 3076

commit v4 on v3

--- a/solution.py
+++ b/solution.py
@@ -30,6 +30,10 @@
         start = first + j * stride
         value = jnp.where(block == j, stacked[start : start + ROWS], value)
     return value
+
+
+def unroll_of(count):
+    return next(k for k in (3, 2, 1) if count % k == 0)
 
 
 def far_kernel(
@@ -65,9 +69,9 @@
     mine = [jnp.where(lane_group == i, 1.0, 0.0).astype(bf16) for i in range(STEP)]
     fill = jnp.zeros((LANES - ROWS, WIDE), f32)
 
-    def step(s, carry):
+    def some(s, rows):
+        count = rows.shape[0]
         row = clists_ref[s]
-        rows = lists_ref[pl.ds(pl.multiple_of(s * STEP, STEP), STEP), :]
         found = jnp.dot(parent_ref[...], one_hot(row % WIDE, WIDE), preferred_element_type=f32)
         high = pick_block(found, row // WIDE, 0, 2 * ROWS, groups)
         low = pick_block(found, row // WIDE, ROWS, 2 * ROWS, groups)
@@ -75,7 +79,7 @@
         high = jnp.concatenate([high, fill], 0).astype(bf16)
         low = jnp.concatenate([low, fill], 0).astype(bf16)
         matrix = []
-        for i in range(STEP):
+        for i in range(count):
             offset = s * STEP + i
             row = rows[i : i + 1]
             found = jnp.dot(source_ref[...], one_hot(row % WIDE, WIDE), preferred_element_type=f32)
@@ -84,13 +88,21 @@
             column_ref[LANES * i : LANES * (i + 1), WIDE:] = (
                 high * mine[i] + low * mine[(i + STEP // 2) % STEP]
             )
-            start = pl.multiple_of(jnp.minimum(offset, offsets - 1) * ROWS, ROWS)
+            start = pl.multiple_of(offset * ROWS, ROWS)
             matrix.append(matrix_ref[pl.ds(start, ROWS), :].astype(bf16))
         matrix = jnp.concatenate(matrix, 1)
-        acc_ref[...] += jnp.dot(matrix, column_ref[...], preferred_element_type=f32)
-        return carry
-
-    lax.fori_loop(0, clists_ref.shape[0], step, 0, unroll=2)
+        acc_ref[...] += jnp.dot(
+            matrix, column_ref[: LANES * count], preferred_element_type=f32
+        )
+
+    def step(s, carry):
+        some(s, lists_ref[pl.ds(pl.multiple_of(s * STEP, STEP), STEP), :])
+        return carry
+
+    full = offsets // STEP
+    lax.fori_loop(0, full, step, 0, unroll=unroll_of(full))
+    if full * STEP < offsets:
+        some(full, lists_ref[full * STEP :, :])
     coarse = acc_ref[:, WIDE : WIDE + LANES] + acc_ref[:, WIDE + LANES :]
     coarse = coarse + pltpu.roll(coarse, LANES // 2, 1)
     coarse = coarse + pltpu.roll(coarse, LANES // 4, 1)
@@ -117,7 +129,6 @@
     groups = source.shape[0] // ROWS - 1
     steps = -(-offsets // STEP)
     extra = ((0, steps * STEP - offsets), (0, 0))
-    lists = jnp.pad(leaf_lists, extra, constant_values=(groups + 1) * WIDE)
     clists = jnp.pad(coarse_lists, extra, constant_values=groups * WIDE).reshape(steps, 1, WIDE)
     vmem = pl.BlockSpec(memory_space=pltpu.VMEM)
     return pl.pallas_call(
@@ -134,13 +145,13 @@
         ],
         compiler_params=pltpu.CompilerParams(vmem_limit_bytes=48 * 2**20),
         name="far",
-    )(source, parents, translate.transpose(1, 2, 0), shift_down, lists, clists)
+    )(source, parents, translate.transpose(1, 2, 0), shift_down, leaf_lists, clists)
 
 
 def exchange_kernel(
     leaf_ref, rows_ref, up_ref, atoms_ref, lists_ref, counts_ref,
     source_ref, parent_ref, near_ref,
-    send_ref, land_ref, edge_ref, side_ref, send_sem, land_sem, edge_send_sem, edge_land_sem,
+    send_ref, land_ref, edge_ref, side_ref, entry_ref, send_sem, land_sem, edge_send_sem, edge_land_sem,
 ):
     coeffs, boxes = leaf_ref.shape
     slots = near_ref.shape[0]
@@ -174,7 +185,8 @@
     low = (up - high.astype(f32)).astype(bf16)
     together = WIDE // CAP
     for j in range(peers // together):
-        hot = one_hot(rows_ref[:, j * WIDE : (j + 1) * WIDE], boxes)
+        named = [rows_ref[p : p + 1, :] for p in range(j * together, (j + 1) * together)]
+        hot = one_hot(jnp.concatenate(named, 1), boxes)
         part = jnp.transpose(jnp.dot(packed, hot, preferred_element_type=f32)).astype(bf16)
         for i in range(together):
             p = j * together + i
@@ -227,12 +239,15 @@
         before = atoms_ref[:, (t - 1) * LANES : t * LANES] if t else below
         side_ref[:, t * LANES : (t + 1) * LANES] = jnp.where(lower, after, before)
 
+    for n in range(lists_ref.shape[0]):
+        entry_ref[n] = lists_ref[n : n + 1, :]
+
     def step(n, totals):
         out = []
         for t in range(tiles):
             lanes = slice(t * LANES, (t + 1) * LANES)
             total = totals[t]
-            entry = lists_ref[n, :, lanes]
+            entry = entry_ref[n, :, lanes]
             local = jnp.broadcast_to(entry - HALO, (8, LANES))
             inside = (local >= t * LANES) & (local < (t + 1) * LANES)
             lane = local & (LANES - 1)
@@ -255,7 +270,9 @@
         return tuple(out)
 
     zero = jnp.zeros((slots, LANES), f32)
-    totals = lax.fori_loop(0, lists_ref.shape[0], step, (zero,) * tiles)
+    totals = lax.fori_loop(
+        0, lists_ref.shape[0], step, (zero,) * tiles, unroll=unroll_of(lists_ref.shape[0])
+    )
     slot = lax.broadcasted_iota(jnp.int32, (slots, LANES), 0)
     for t in range(tiles):
         lanes = slice(t * LANES, (t + 1) * LANES)
@@ -309,6 +326,7 @@
             pltpu.VMEM((peers, 3 * CAP, LANES), bf16),
             pltpu.VMEM((2, 4 * slots, LANES), f32),
             pltpu.VMEM((4 * slots, boxes), f32),
+            pltpu.VMEM((near_lists.shape[0], 1, boxes), jnp.int32),
             pltpu.SemaphoreType.DMA((peers,)),
             pltpu.SemaphoreType.DMA((peers,)),
             pltpu.SemaphoreType.DMA((2,)),
@@ -319,8 +337,8 @@
         ),
         name="exchange",
     )(
-        leaf_multipoles, export_rows.reshape(1, peers * CAP), parents, atoms,
-        near_lists[:, None, :], counts[None, :],
+        leaf_multipoles, export_rows[0], parents, atoms,
+        near_lists, counts[None, :],
     )
     return source, parent, potential.T.reshape(boxes * slots)
 

time: 58.8 us -> 57.2 us (0.973)
  Pallas kernels: 46.5 us -> 45 us
    unnamed x9 -> x15, local copies, waits for them, and re-layouts: 4.24 us -> 6.66 us
    pallas_call x1, Pallas kernels: 15.8 us -> 14.2 us  [exchange(): pl.pallas_call(exchange_kernel, out_shape=(jax.ShapeDtypeStruct(((groups...]
    pad x1 -> x0, local copies, waits for them, and re-layouts: 1 us -> none  [far_sum(): lists = jnp.pad(leaf_lists, extra, constant_values=(groups + 1) * WIDE)]
    broadcast_in_dim x1 -> x0, local copies, waits for them, and re-layouts: 0.78 us -> none  [exchange(): near_lists[:, None, :]]
    reshape x1 -> x0, local copies, waits for them, and re-layouts: 0.78 us -> none  [exchange(): export_rows.reshape(1, peers * CAP)]
where the time goes in v4:
time: 57.2 us; the launch traced here: 56.3 us
  Pallas kernels  45 us (79%)
  local copies, waits for them, and re-layouts  9.67 us (17%)
  between operations  0.73 us (1%)
  other arithmetic  0.7 us (1%)
    pallas_call x1, Pallas kernels, far_sum(): pl.pallas_call(far_kernel, out_shape=jax.ShapeDtypeStruct((coeffs, boxes)...  30.8 us
    pallas_call x1, Pallas kernels, exchange(): pl.pallas_call(exchange_kernel, out_shape=(jax.ShapeDtypeStruct(((groups...  14.2 us
    unnamed x15, local copies, waits for them, and re-layouts  6.66 us

profile of v4, /device:TPU:1, one launch (start us, length us, event | category | flops | bytes accessed | tf_op | source)
XLA Modules:
  0.0 56.3 jit_solution(6673069524522607305)
XLA Ops:
  0.6 0.0 copy-start
  0.6 1.0 %reshape.24 = f32[3,256,16]{2,1,0:T(8,128)S(1)} reshape(f32[3,4096]{1,0:T(4,128)} %param.18) | data formatting | bytes 98304 | tf_op jit(solution)/shard_map/reshape | solution.py:312
  1.7 0.1 copy.21
  1.8 0.8 %reshape.26 = f32[256,16]{1,0:T(8,128)S(1)} reshape(f32[4096]{0:T(1024)} %param.19) | data formatting | bytes 32768 | tf_op jit(solution)/shard_map/reshape | solution.py:311
  2.6 0.1 copy.22
  2.7 0.7 %bitcast_select_fusion = f32[16,256]{1,0:T(8,128)S(1)} fusion(f32[256,16]{0,1:T(8,128)S(1)} %copy.22, s32[256]{0:T(256)} %param.20), kind=kLoop, calls=%fused_computation.4 | loop fusion | flops 8192 | bytes 33792 | tf_op jit(solution)/shard_map/jit(_where)/select_n | solution.py:311
  3.4 0.9 %copy.18 = bf16[81,256]{0,1:T(8,128)(2,1)S(1)} copy(bf16[81,256]{1,0:T(8,128)(2,1)} %leaf_ref.1) | data formatting | bytes 82944 | tf_op args[0]
  4.3 0.0 copy-done
  4.3 0.2 convolution_bitcast_fusion
  4.5 0.0 copy-start.2
  4.5 0.8 %copy-done.2 = bf16[81,256]{1,0:T(8,128)(2,1)S(1)} copy-done((bf16[81,256]{1,0:T(8,128)(2,1)S(1)}, bf16[81,256]{1,0:T(8,128)(2,1)}, u32[]{:S(2)}) %copy-start.2) | copy-done | bytes 41496
  5.3 0.0 copy-start.3
  5.3 0.8 %copy-done.3 = s32[27,256]{1,0:T(8,128)S(1)} copy-done((s32[27,256]{1,0:T(8,128)S(1)}, s32[27,256]{1,0:T(8,128)}, u32[]{:S(2)}) %copy-start.3) | copy-done | bytes 27672
  6.1 0.0 copy-start.4
  6.1 0.7 %copy-done.4 = s32[1,16,32]{2,1,0:T(8,128)S(1)} copy-done((s32[1,16,32]{2,1,0:T(8,128)S(1)}, s32[1,16,32]{2,1,0:T(8,128)}, u32[]{:S(2)}) %copy-start.4) | copy-done | bytes 2072
  6.8 0.0 copy-start.5
  6.8 0.7 %copy-done.5 = s32[256]{0:T(256)S(1)} copy-done((s32[256]{0:T(256)S(1)}, s32[256]{0:T(256)}, u32[]{:S(2)}) %copy-start.5) | copy-done | bytes 1048
  7.4 14.2 %exchange.1 = (bf16[264,256]{1,0:T(8,128)(2,1)S(1)}, bf16[352,256]{1,0:T(8,128)(2,1)S(1)}, f32[16,256]{1,0:T(8,128)S(1)}) custom-call(bf16[81,256]{1,0:T(8,128)(2,1)S(1)} %copy-done.2, s32[16,32]{1,0:T(8,128)S(1)} %bitcast.12, f32[32,128]{1,0:T(8,128)S(1)} %pad.8.up_ref, f32[64,256]{1,0:T(8,128)S(1)} %pad_maximum_fusion.atoms_ref, s32[27,256]{1,0:T(8,128)S(1)} %copy-done.3, ...), custom_call_target="tpu_custom_call" | custom-call | tf_op jit(solution)/shard_map/exchange/pallas_call | solution.py:315
  21.7 0.9 %copy.27 = s32[316,32]{1,0:T(8,128)S(1)} copy(s32[316,32]{0,1:T(8,128)} %param.17) | data formatting | bytes 80896
  22.6 0.1 reshape.30.clists_ref
  22.8 0.9 %copy.24.down_ref = bf16[8,81,81]{2,1,0:T(8,128)(2,1)S(1)} copy(bf16[8,81,81]{2,0,1:T(8,128)(2,1)} %param.14) | data formatting | bytes 209952 | tf_op args[3]
  23.7 0.0 copy-start.1
  23.7 1.0 %copy-done.1 = s32[316,256]{1,0:T(8,128)S(1)} copy-done((s32[316,256]{1,0:T(8,128)S(1)}, s32[316,256]{1,0:T(8,128)}, u32[]{:S(2)}) %copy-start.1) | copy-done | bytes 323608
  24.7 30.8 %far.1 = f32[81,256]{1,0:T(8,128)} custom-call(bf16[264,256]{1,0:T(8,128)(2,1)S(1)} %get-tuple-element.5.source_ref, bf16[352,256]{1,0:T(8,128)(2,1)S(1)} %get-tuple-element.6.parent_ref, bf16[81,81,316]{2,1,0:T(8,128)(2,1)} %bitcast.14, bf16[8,81,81]{2,1,0:T(8,128)(2,1)S(1)} %copy.24.down_ref, s32[316,256]{1,0:T(8,128)S(1)} %copy-done.1, ...), custom_call_target="tpu_custom_call" | custom-call | tf_op jit(solution)/shard_map/far/pallas_call | solution.py:134
  55.5 0.1 copy.26
  55.6 0.7 %reshape.28 = f32[4096]{0:T(1024)} reshape(f32[256,16]{1,0:T(8,128)S(1)} %copy.26) | data formatting | bytes 32768 | tf_op jit(solution)/shard_map/reshape | solution.py:343
  (3 shorter events, 0.0 us)
Async XLA Ops:
  0.6 3.7 %copy-start = (bf16[8,81,81]{2,0,1:T(8,128)(2,1)S(1)}, bf16[8,81,81]{2,0,1:T(8,128)(2,1)}, u32[]{:S(2)}) copy-start(bf16[8,81,81]{2,0,1:T(8,128)(2,1)} %param.13) | copy-start | bytes 314932
  4.5 0.8 %copy-start.2 = (bf16[81,256]{1,0:T(8,128)(2,1)S(1)}, bf16[81,256]{1,0:T(8,128)(2,1)}, u32[]{:S(2)}) copy-start(bf16[81,256]{1,0:T(8,128)(2,1)} %leaf_ref.1) | copy-start | bytes 124420
  5.3 0.8 %copy-start.3 = (s32[27,256]{1,0:T(8,128)S(1)}, s32[27,256]{1,0:T(8,128)}, u32[]{:S(2)}) copy-start(s32[27,256]{1,0:T(8,128)} %lists_ref.2) | copy-start | bytes 82948
  6.1 0.7 %copy-start.4 = (s32[1,16,32]{2,1,0:T(8,128)S(1)}, s32[1,16,32]{2,1,0:T(8,128)}, u32[]{:S(2)}) copy-start(s32[1,16,32]{2,1,0:T(8,128)} %param.15) | copy-start | bytes 6148
  6.8 0.7 %copy-start.5 = (s32[256]{0:T(256)S(1)}, s32[256]{0:T(256)}, u32[]{:S(2)}) copy-start(s32[256]{0:T(256)} %param.20) | copy-start | bytes 3076
  23.7 1.0 %copy-start.1 = (s32[316,256]{1,0:T(8,128)S(1)}, s32[316,256]{1,0:T(8,128)}, u32[]{:S(2)}) copy-start(s32[316,256]{1,0:T(8,128)} %lists_ref.3) | copy-start | bytes 970756

commit v5 on v4

--- a/solution.py
+++ b/solution.py
@@ -10,6 +10,7 @@
 LANES = 128
 WIDE = 256
 ROWS = 88
+KEPT = 96
 STEP = 8
 
 softening = 0.01
@@ -53,6 +54,7 @@
     for j in range(pieces):
         fetch(j).start()
     acc_ref[...] = jnp.zeros_like(acc_ref)
+    column_ref[...] = jnp.zeros_like(column_ref)
 
     def turn(j, carry):
         fetch(j).wait()
@@ -67,7 +69,7 @@
     lax.fori_loop(0, pieces, turn, 0)
     lane_group = lax.broadcasted_iota(jnp.int32, (1, WIDE), 1) // (WIDE // STEP)
     mine = [jnp.where(lane_group == i, 1.0, 0.0).astype(bf16) for i in range(STEP)]
-    fill = jnp.zeros((LANES - ROWS, WIDE), f32)
+    fill = jnp.zeros((KEPT - ROWS, WIDE), f32)
 
     def some(s, rows):
         count = rows.shape[0]
@@ -84,8 +86,8 @@
             row = rows[i : i + 1]
             found = jnp.dot(source_ref[...], one_hot(row % WIDE, WIDE), preferred_element_type=f32)
             column = pick_block(found, row // WIDE, 0, ROWS, groups + 1)
-            column_ref[LANES * i : LANES * (i + 1), :WIDE] = jnp.concatenate([column, fill], 0).astype(bf16)
-            column_ref[LANES * i : LANES * (i + 1), WIDE:] = (
+            column_ref[LANES * i : LANES * i + KEPT, :WIDE] = jnp.concatenate([column, fill], 0).astype(bf16)
+            column_ref[LANES * i : LANES * i + KEPT, WIDE:] = (
                 high * mine[i] + low * mine[(i + STEP // 2) % STEP]
             )
             start = pl.multiple_of(offset * ROWS, ROWS)
@@ -143,7 +145,7 @@
             pltpu.VMEM((ROWS, 2 * WIDE), f32),
             pltpu.SemaphoreType.DMA((9 if coeffs % 9 == 0 else 1,)),
         ],
-        compiler_params=pltpu.CompilerParams(vmem_limit_bytes=48 * 2**20),
+        compiler_params=pltpu.CompilerParams(vmem_limit_bytes=58 * 2**20),
         name="far",
     )(source, parents, translate.transpose(1, 2, 0), shift_down, leaf_lists, clists)
 
@@ -333,7 +335,7 @@
             pltpu.SemaphoreType.DMA((2,)),
         ],
         compiler_params=pltpu.CompilerParams(
-            collective_id=0, has_side_effects=True, vmem_limit_bytes=32 * 2**20
+            collective_id=0, has_side_effects=True, vmem_limit_bytes=58 * 2**20
         ),
         name="exchange",
     )(

time: 57.2 us -> 57.8 us (1.010)
  local copies, waits for them, and re-layouts: 9.67 us -> 7.69 us
  Pallas kernels: 45 us -> 46.9 us
  other arithmetic: 0.7 us -> 1.33 us
    unnamed x15 -> x7, local copies, waits for them, and re-layouts: 6.66 us -> 3.44 us
    pallas_call x1, Pallas kernels: 14.2 us -> 15.7 us  [exchange(): pl.pallas_call(exchange_kernel, out_shape=(jax.ShapeDtypeStruct(((groups...]
    concatenate x1, other arithmetic: 0.01 us -> 0.64 us  [exchange(): atoms = jnp.concatenate([place, charge], 0)]
    reshape x1, local copies, waits for them, and re-layouts: 0.13 us -> 0.74 us  [far_sum(): jnp.pad(coarse_lists, extra, constant_values=groups * WIDE)]
    pad x1, local copies, waits for them, and re-layouts: 0.02 us -> 0.64 us  [exchange(): parents = jnp.pad(parents, ((0, 0), (0, LANES - coeffs)))]
where the time goes in v5:
time: 57.8 us; the launch traced here: 56.8 us
  Pallas kernels  46.9 us (81%)
  local copies, waits for them, and re-layouts  7.69 us (13%)
  other arithmetic  1.33 us (2%)
  between operations  0.71 us (1%)
    pallas_call x1, Pallas kernels, far_sum(): pl.pallas_call(far_kernel, out_shape=jax.ShapeDtypeStruct((coeffs, boxes)...  31.2 us
    pallas_call x1, Pallas kernels, exchange(): pl.pallas_call(exchange_kernel, out_shape=(jax.ShapeDtypeStruct(((groups...  15.7 us
    unnamed x7, local copies, waits for them, and re-layouts  3.44 us

profile of v5, /device:TPU:1, one launch (start us, length us, event | category | flops | bytes accessed | tf_op | source)
XLA Modules:
  0.0 56.8 jit_solution(7709077004969130492)
XLA Ops:
  0.6 0.0 copy-start
  0.6 1.0 %reshape.24 = f32[3,256,16]{2,1,0:T(8,128)S(1)} reshape(f32[3,4096]{1,0:T(4,128)} %param.18) | data formatting | bytes 98304 | tf_op jit(solution)/shard_map/reshape | solution.py:314
  1.7 0.1 copy.21
  1.8 0.8 %reshape.26 = f32[256,16]{1,0:T(8,128)S(1)} reshape(f32[4096]{0:T(1024)} %param.19) | data formatting | bytes 32768 | tf_op jit(solution)/shard_map/reshape | solution.py:313
  2.6 0.1 copy.22
  2.7 0.7 %bitcast_select_fusion = f32[16,256]{1,0:T(8,128)S(1)} fusion(f32[256,16]{0,1:T(8,128)S(1)} %copy.22, s32[256]{0:T(256)} %param.20), kind=kLoop, calls=%fused_computation.4 | loop fusion | flops 8192 | bytes 33792 | tf_op jit(solution)/shard_map/jit(_where)/select_n | solution.py:313
  3.4 0.6 %pad_maximum_fusion.atoms_ref = f32[64,256]{1,0:T(8,128)} fusion(f32[16,256]{1,0:T(8,128)S(1)} %bitcast_select_fusion, f32[48,256]{1,0:T(8,128)S(1)} %bitcast.14), kind=kLoop, calls=%fused_computation.2 | loop fusion | flops 16384 | bytes 131072 | tf_op jit(solution)/shard_map/concatenate | solution.py:315
  4.0 0.9 %copy.18 = bf16[81,256]{0,1:T(8,128)(2,1)S(1)} copy(bf16[81,256]{1,0:T(8,128)(2,1)} %leaf_ref.1) | data formatting | bytes 82944 | tf_op args[0]
  5.0 0.0 copy-done
  5.0 0.2 convolution_bitcast_fusion
  5.1 0.6 %pad.8.up_ref = f32[32,128]{1,0:T(8,128)} pad(f32[32,81]{1,0:T(8,128)S(1)} %convolution_bitcast_fusion, f32[]{:T(128)} %constant.2.clone.1), padding=0_0x0_47 | pad | bytes 26756 | tf_op jit(solution)/shard_map/jit(_pad)/pad | solution.py:311
  5.8 15.7 %exchange.1 = (bf16[264,256]{1,0:T(8,128)(2,1)}, bf16[352,256]{1,0:T(8,128)(2,1)}, f32[16,256]{1,0:T(8,128)}) custom-call(bf16[81,256]{1,0:T(8,128)(2,1)} %leaf_ref.1, s32[16,32]{1,0:T(8,128)} %bitcast.16, f32[32,128]{1,0:T(8,128)} %pad.8.up_ref, f32[64,256]{1,0:T(8,128)} %pad_maximum_fusion.atoms_ref, s32[27,256]{1,0:T(8,128)} %lists_ref.2, s32[1,256]{1,0:T(1,128)} %bitcast.17), custom_call_target="tpu_custom_call" | custom-call | tf_op jit(solution)/shard_map/exchange/pallas_call | solution.py:317
  21.5 0.0 copy-start.1
  21.5 0.9 %copy.27 = s32[316,32]{1,0:T(8,128)S(1)} copy(s32[316,32]{0,1:T(8,128)} %param.17) | data formatting | bytes 80896
  22.4 0.7 %reshape.30.clists_ref = s32[40,1,256]{2,1,0:T(1,128)} reshape(s32[320,32]{1,0:T(8,128)S(1)} %pad.9.clone) | data formatting | bytes 81920 | tf_op jit(solution)/shard_map/reshape | solution.py:134
  23.2 1.6 %copy.24.down_ref = bf16[8,81,81]{2,1,0:T(8,128)(2,1)} copy(bf16[8,81,81]{2,0,1:T(8,128)(2,1)} %param.14) | data formatting | bytes 209952 | tf_op args[3]
  24.8 31.2 %far.1 = f32[81,256]{1,0:T(8,128)} custom-call(bf16[264,256]{1,0:T(8,128)(2,1)} %get-tuple-element.5.source_ref, bf16[352,256]{1,0:T(8,128)(2,1)} %get-tuple-element.6.parent_ref, bf16[81,81,316]{2,1,0:T(8,128)(2,1)} %bitcast.11, bf16[8,81,81]{2,1,0:T(8,128)(2,1)} %copy.24.down_ref, s32[316,256]{1,0:T(8,128)} %lists_ref.3, s32[40,1,256]{2,1,0:T(1,128)} %reshape.30.clists_ref), custom_call_target="tpu_custom_call" | custom-call | tf_op jit(solution)/shard_map/far/pallas_call | solution.py:136
  56.0 0.0 copy-done.1
  56.0 0.1 copy.26
  56.1 0.7 %reshape.28 = f32[4096]{0:T(1024)} reshape(f32[256,16]{1,0:T(8,128)S(1)} %copy.26) | data formatting | bytes 32768 | tf_op jit(solution)/shard_map/reshape | solution.py:345
  (1 shorter events, 0.0 us)
Async XLA Ops:
  0.6 4.3 %copy-start = (bf16[8,81,81]{2,0,1:T(8,128)(2,1)S(1)}, bf16[8,81,81]{2,0,1:T(8,128)(2,1)}, u32[]{:S(2)}) copy-start(bf16[8,81,81]{2,0,1:T(8,128)(2,1)} %param.13) | copy-start | bytes 314932
  21.5 34.5 %copy-start.1 = (f32[16,256]{1,0:T(8,128)S(1)}, f32[16,256]{1,0:T(8,128)}, u32[]{:S(2)}) copy-start(f32[16,256]{1,0:T(8,128)} %get-tuple-element.7) | copy-start | bytes 49156
